TPU v7x, 128 devices: a whole 4x4x4 slice. The times are simulated.
128 devices in a mesh: outer: 32 (over z, y, core), inner: 4 (over x).
Axes of the slice: x: 4, y: 4, z: 4, core: 2. Of those that a mesh axis runs over, the one named last changes fastest.
Arguments:
- x_in: bfloat16 [16384, 8192], P(('outer', 'inner')), may hold values from -6 to 6
- gate_in: bfloat16 [16384, 8192], P(('outer', 'inner')), may hold values from -6 to 6
- conv_weight: float32 [4, 8192], replicated, may hold values from -3 to 3
- conv_bias: float32 [8192], replicated, may hold values from -3 to 3
- x_proj: bfloat16 [8192, 288], replicated, may hold values from -0.0625 to 0.0625
- dt_proj: bfloat16 [256, 8192], replicated, may hold values from -0.375 to 0.375
- dt_bias: float32 [8192], replicated, may hold values from -9 to -2
- decay_rates: float32 [16, 8192], replicated, may hold values from 1 to 16
- skip_gain: float32 [8192], replicated, may hold values from 0.5 to 1.5
Outputs:
- gated_out: bfloat16 [16384, 8192], P(('outer', 'inner'))
All inputs are finite; a program needn't handle non-finite values.
Results may differ from a plain program's by a relative error of at most 0.0085.
Values may be sent and summed in bfloat16 or wider, within the bound.
A program may use at most 192 MiB of HBM per device.

v0:
```python
import jax
import jax.numpy as jnp
from jax import lax
from jax.sharding import Mesh
from jax.sharding import PartitionSpec as P

OUTER_INNER = ("outer_0", "outer_1", "outer_2", "inner")


dt_ceiling = 0.25


def shifted(value, axis, steps):
    count = lax.axis_size(axis)
    initial, last = (max(0, -steps), min(count, count - steps))
    return lax.ppermute(value, axis, [(source, source + steps) for source in range(initial, last)])


def neutral_like(value, identity):
    return jax.tree.map(
        lambda a, e: jnp.broadcast_to(jnp.asarray(e, a.dtype), a.shape), value, identity
    )


def prefix_by_axis(value, axes, combine, identity):
    before = start = neutral_like(value, identity)
    running = value
    for axis in reversed(axes):
        peers, here = (lax.axis_size(axis), lax.axis_index(axis))
        pieces = jax.tree.map(lambda part: lax.all_gather(part, axis), running)
        inside, running = (start, start)
        for k in range(peers):
            passed = k < here
            running = combine(running, jax.tree.map(lambda part: part[k], pieces))
            inside = jax.tree.map(lambda new, old: jnp.where(passed, new, old), running, inside)
        before = combine(inside, before)
    return before


def local(x_in, gate_in, conv_weight, conv_bias, x_proj, dt_proj, dt_bias, decay_rates, skip_gain):
    rows = x_in.shape[0]
    width = x_in.shape[1]
    taps = conv_weight.shape[0]
    rank = dt_proj.shape[0]
    states = decay_rates.shape[0]
    tail = x_in[rows - (taps - 1) :]
    prior = shifted(tail, OUTER_INNER, 1)
    padded = jnp.concatenate([prior, x_in], axis=0).astype(jnp.float32)
    conv = conv_bias[None, :]
    for k in range(taps):
        conv = conv + conv_weight[k][None, :] * padded[k : k + rows]
    u_act = jax.nn.silu(conv).astype(jnp.bfloat16)
    proj = jnp.dot(u_act, x_proj, preferred_element_type=jnp.float32)
    dt_low = proj[:, :rank].astype(jnp.bfloat16)
    bmat = proj[:, rank : rank + states]
    cmat = proj[:, rank + states :]
    step_size = jnp.minimum(
        jax.nn.softplus(
            jnp.dot(dt_low, dt_proj, preferred_element_type=jnp.float32) + dt_bias[None, :]
        ),
        dt_ceiling,
    )
    ufloat = u_act.astype(jnp.float32)
    block = 16
    blocks = rows // block
    dt_blocks = step_size.reshape(blocks, block, width)
    in_blocks = (step_size * ufloat).reshape(blocks, block, width)
    b_blocks = bmat.reshape(blocks, block, states)
    c_blocks = cmat.reshape(blocks, block, states)

    def block_step(carry, inputs):
        state, offset = carry
        dt_blk, in_blk, b_blk, c_blk = inputs
        cumul = jnp.cumsum(dt_blk, axis=0)
        growth = cumul[:, None, :] * decay_rates[None, :, :]
        weighted = jnp.exp(growth) * b_blk[:, :, None] * in_blk[:, None, :]
        running = jnp.cumsum(weighted, axis=0)
        series = jnp.exp(-growth) * (state[None, :, :] + running)
        whole_cum = cumul + offset[None, :]
        return (
            (series[-1], whole_cum[-1]),
            (jnp.sum(c_blk[:, :, None] * series, axis=1), whole_cum),
        )

    start = (jnp.zeros((states, width), jnp.float32), jnp.zeros((width,), jnp.float32))
    finals, outs_pair = lax.scan(block_step, start, (dt_blocks, in_blocks, b_blocks, c_blocks))
    local_state, dt_total = finals
    local_out = outs_pair[0].reshape(rows, width)
    cum_blocks = outs_pair[1]
    neutral = (jnp.zeros((width,), jnp.float32), jnp.zeros((states, width), jnp.float32))

    def combine(earlier, later):
        return (
            earlier[0] + later[0],
            jnp.exp(-later[0][None, :] * decay_rates) * earlier[1] + later[1],
        )

    incoming = prefix_by_axis((dt_total, local_state), OUTER_INNER, combine, neutral)
    carry_state = incoming[1]

    def correction(inputs):
        c_blk, cum_blk = inputs
        faded = jnp.exp(-cum_blk[:, None, :] * decay_rates[None, :, :]) * carry_state[None, :, :]
        return jnp.sum(c_blk[:, :, None] * faded, axis=1)

    fixed = lax.map(correction, (c_blocks, cum_blocks)).reshape(rows, width)
    y_full = local_out + fixed + skip_gain[None, :] * ufloat
    return (y_full * jax.nn.silu(gate_in.astype(jnp.float32))).astype(jnp.bfloat16)


def solution(mesh):
    finer = Mesh(
        mesh.devices.reshape(4, 4, 2, mesh.shape["inner"]),
        ("outer_0", "outer_1", "outer_2", "inner"),
    )
    return jax.shard_map(
        local,
        mesh=finer,
        in_specs=(P(OUTER_INNER, None), P(OUTER_INNER, None), P(), P(), P(), P(), P(), P(), P()),
        out_specs=P(OUTER_INNER, None),
        check_vma=False,
    )
```

profile of v0, /device:TPU:1, one launch (start us, length us, event | category | flops | bytes accessed | tf_op | source)
XLA Modules:
  0.0 280.3 jit_solution(17429097215463025956)
XLA Ops:
  7.5 3.9 %collective-permute-start = (bf16[3,8192]{1,0:T(4,128)(2,1)S(1)}, bf16[3,8192]{1,0:T(4,128)(2,1)S(1)}, u32[]{:S(2)}, u32[]{:S(2)}) collective-permute-start(bf16[3,8192]{1,0:T(4,128)(2,1)S(1)} %slice.128), channel_id=1, source_target_pairs={{0,1},{1,2},{2,3},{3,4},{4,5},{5,6},{6,7},{7,8},{8,9},{9,10},{10,1... | collective-permute-start | bytes 147464 | tf_op jit(solution)/shard_map/ppermute | solution.py:16
  17.6 2.7 multiply_convert_fusion
  22.1 8.7 %convert_multiply_fusion.2 = (f32[128,8192]{1,0:T(8,128)}, f32[128,8192]{1,0:T(8,128)}) fusion(bf16[128,8192]{1,0:T(8,128)(2,1)S(1)} %multiply_convert_fusion, f32[8192]{0:T(1024)S(1)} %copy-done.22, bf16[256,8192]{1,0:T(8,128)(2,1)} %param.18, f32[128,288]{0,1:T(8,128)S(1)} %fusion.31), kind=kOutput, calls=%fused_computation.30 | convolution fusion | flops 547356672 | bytes 14778368 | tf_op jit(solution)/shard_map/dot_general | solution.py:59
  35.6 67.7 %while.26 = (s32[]{:T(128)}, f32[16,8192]{1,0:T(8,128)S(1)}, f32[8192]{0:T(1024)S(1)}, f32[8,16,8192]{2,1,0:T(8,128)}, f32[8,16,8192]{2,1,0:T(8,128)}, /*index=5...) while((s32[]{:T(128)}, f32[16,8192]{1,0:T(8,128)S(1)}, ...), condition=%wide.region_4.5_spmd, body=%wide.region_0.4_spmd.sunk | while | flops 52305920 | bytes 17504404 | solution.py:86
  38.3 4.6 %multiply_reduce_fusion.4 = (f32[16,8192]{1,0:T(8,128)S(1)}, f32[16,16,8192]{2,1,0:T(8,128)S(1)}) fusion(f32[16,16]{1,0:T(8,128)S(1)} %dynamic-slice_bitcast_fusion.10, f32[16,8192]{1,0:T(8,128)S(1)} %dynamic-slice_bitcast_fusion.11, f32[16,16]{1,0:T(8,128)S(1)} %dynamic-slice_bitcast_fusion.12, f32[16,8192]{1,0:T(8,128)S(1)} %get-tuple-element.347, ...), kind=kOutput, calls=%fused_computation.7.clone.1 | output fusion | flops 50200576 | bytes 11012096 | tf_op jit(solution)/shard_map/while/body/eval_jaxpr/jit(cumsum)/reduce_window_sum | solution.py:77
  46.8 4.6 %multiply_reduce_fusion.4 = (f32[16,8192]{1,0:T(8,128)S(1)}, f32[16,16,8192]{2,1,0:T(8,128)S(1)}) fusion(f32[16,16]{1,0:T(8,128)S(1)} %dynamic-slice_bitcast_fusion.10, f32[16,8192]{1,0:T(8,128)S(1)} %dynamic-slice_bitcast_fusion.11, f32[16,16]{1,0:T(8,128)S(1)} %dynamic-slice_bitcast_fusion.12, f32[16,8192]{1,0:T(8,128)S(1)} %get-tuple-element.347, ...), kind=kOutput, calls=%fused_computation.7.clone.1 | output fusion | flops 50200576 | bytes 11012096 | tf_op jit(solution)/shard_map/while/body/eval_jaxpr/jit(cumsum)/reduce_window_sum | solution.py:77
  55.2 4.6 %multiply_reduce_fusion.4 = (f32[16,8192]{1,0:T(8,128)S(1)}, f32[16,16,8192]{2,1,0:T(8,128)S(1)}) fusion(f32[16,16]{1,0:T(8,128)S(1)} %dynamic-slice_bitcast_fusion.10, f32[16,8192]{1,0:T(8,128)S(1)} %dynamic-slice_bitcast_fusion.11, f32[16,16]{1,0:T(8,128)S(1)} %dynamic-slice_bitcast_fusion.12, f32[16,8192]{1,0:T(8,128)S(1)} %get-tuple-element.347, ...), kind=kOutput, calls=%fused_computation.7.clone.1 | output fusion | flops 50200576 | bytes 11012096 | tf_op jit(solution)/shard_map/while/body/eval_jaxpr/jit(cumsum)/reduce_window_sum | solution.py:77
  63.7 4.6 %multiply_reduce_fusion.4 = (f32[16,8192]{1,0:T(8,128)S(1)}, f32[16,16,8192]{2,1,0:T(8,128)S(1)}) fusion(f32[16,16]{1,0:T(8,128)S(1)} %dynamic-slice_bitcast_fusion.10, f32[16,8192]{1,0:T(8,128)S(1)} %dynamic-slice_bitcast_fusion.11, f32[16,16]{1,0:T(8,128)S(1)} %dynamic-slice_bitcast_fusion.12, f32[16,8192]{1,0:T(8,128)S(1)} %get-tuple-element.347, ...), kind=kOutput, calls=%fused_computation.7.clone.1 | output fusion | flops 50200576 | bytes 11012096 | tf_op jit(solution)/shard_map/while/body/eval_jaxpr/jit(cumsum)/reduce_window_sum | solution.py:77
  72.2 4.6 %multiply_reduce_fusion.4 = (f32[16,8192]{1,0:T(8,128)S(1)}, f32[16,16,8192]{2,1,0:T(8,128)S(1)}) fusion(f32[16,16]{1,0:T(8,128)S(1)} %dynamic-slice_bitcast_fusion.10, f32[16,8192]{1,0:T(8,128)S(1)} %dynamic-slice_bitcast_fusion.11, f32[16,16]{1,0:T(8,128)S(1)} %dynamic-slice_bitcast_fusion.12, f32[16,8192]{1,0:T(8,128)S(1)} %get-tuple-element.347, ...), kind=kOutput, calls=%fused_computation.7.clone.1 | output fusion | flops 50200576 | bytes 11012096 | tf_op jit(solution)/shard_map/while/body/eval_jaxpr/jit(cumsum)/reduce_window_sum | solution.py:77
  80.7 4.6 %multiply_reduce_fusion.4 = (f32[16,8192]{1,0:T(8,128)S(1)}, f32[16,16,8192]{2,1,0:T(8,128)S(1)}) fusion(f32[16,16]{1,0:T(8,128)S(1)} %dynamic-slice_bitcast_fusion.10, f32[16,8192]{1,0:T(8,128)S(1)} %dynamic-slice_bitcast_fusion.11, f32[16,16]{1,0:T(8,128)S(1)} %dynamic-slice_bitcast_fusion.12, f32[16,8192]{1,0:T(8,128)S(1)} %get-tuple-element.347, ...), kind=kOutput, calls=%fused_computation.7.clone.1 | output fusion | flops 50200576 | bytes 11012096 | tf_op jit(solution)/shard_map/while/body/eval_jaxpr/jit(cumsum)/reduce_window_sum | solution.py:77
  89.2 4.6 %multiply_reduce_fusion.4 = (f32[16,8192]{1,0:T(8,128)S(1)}, f32[16,16,8192]{2,1,0:T(8,128)S(1)}) fusion(f32[16,16]{1,0:T(8,128)S(1)} %dynamic-slice_bitcast_fusion.10, f32[16,8192]{1,0:T(8,128)S(1)} %dynamic-slice_bitcast_fusion.11, f32[16,16]{1,0:T(8,128)S(1)} %dynamic-slice_bitcast_fusion.12, f32[16,8192]{1,0:T(8,128)S(1)} %get-tuple-element.347, ...), kind=kOutput, calls=%fused_computation.7.clone.1 | output fusion | flops 50200576 | bytes 11012096 | tf_op jit(solution)/shard_map/while/body/eval_jaxpr/jit(cumsum)/reduce_window_sum | solution.py:77
  97.6 4.6 %multiply_reduce_fusion.4 = (f32[16,8192]{1,0:T(8,128)S(1)}, f32[16,16,8192]{2,1,0:T(8,128)S(1)}) fusion(f32[16,16]{1,0:T(8,128)S(1)} %dynamic-slice_bitcast_fusion.10, f32[16,8192]{1,0:T(8,128)S(1)} %dynamic-slice_bitcast_fusion.11, f32[16,16]{1,0:T(8,128)S(1)} %dynamic-slice_bitcast_fusion.12, f32[16,8192]{1,0:T(8,128)S(1)} %get-tuple-element.347, ...), kind=kOutput, calls=%fused_computation.7.clone.1 | output fusion | flops 50200576 | bytes 11012096 | tf_op jit(solution)/shard_map/while/body/eval_jaxpr/jit(cumsum)/reduce_window_sum | solution.py:77
  104.3 9.7 %all-gather = f32[32768]{0:T(1024)S(1)} all-gather(f32[8192]{0:T(1024)S(1)} %get-tuple-element.94), channel_id=2, replica_groups=mesh['outer_0'=4,'outer_1'=4,'outer_2'=2,'inner'=4] {'inner'}, dimensions={0}, use_global_device_ids=true | all-gather | bytes 163840 | tf_op jit(solution)/shard_map/all_gather | solution.py:30
  114.6 4.4 %all-gather.5 = f32[2,1,8192]{2,1,0:T(1,128)S(1)} all-gather(f32[1,1,8192]{2,1,0:T(1,128)S(1)} %bitcast.114), channel_id=1, replica_groups=mesh['outer_0'=4,'outer_1'=4,'outer_2'=2,'inner'=4] {'outer_2'}, dimensions={0}, use_global_device_ids=true | all-gather | bytes 98304 | tf_op jit(solution)/shard_map/all_gather | solution.py:30
  119.0 17.8 %all-gather.13.cloned.1.call-done = f32[64,8192]{1,0:T(8,128)} async-done(((f32[16,8192]{1,0:T(8,128)}), f32[64,8192]{1,0:T(8,128)}) %all-gather.13.cloned.1.call-update) | async-done | bytes 2097168 | tf_op jit(solution)/shard_map/all_gather | solution.py:30
  140.8 9.4 %all-gather.6 = f32[4,1,8192]{2,1,0:T(1,128)S(1)} all-gather(f32[1,1,8192]{2,1,0:T(1,128)S(1)} %get-tuple-element.205), channel_id=1, replica_groups=mesh['outer_0'=4,'outer_1'=4,'outer_2'=2,'inner'=4] {'outer_1'}, dimensions={0}, use_global_device_ids=true | all-gather | bytes 163840 | tf_op jit(solution)/shard_map/all_gather | solution.py:30
  156.5 29.5 %all-gather.17.cloned.1.call-done = f32[64,8192]{1,0:T(8,128)} async-done(((f32[16,8192]{1,0:T(8,128)}), f32[64,8192]{1,0:T(8,128)}) %all-gather.17.cloned.1.call-update) | async-done | bytes 2097168 | tf_op jit(solution)/shard_map/all_gather | solution.py:30
  186.0 2.7 slice_add_fusion.5
  189.5 9.9 %all-gather.7 = f32[4,1,8192]{2,1,0:T(1,128)S(1)} all-gather(f32[1,1,8192]{2,1,0:T(1,128)} %get-tuple-element.190), channel_id=1, replica_groups=mesh['outer_0'=4,'outer_1'=4,'outer_2'=2,'inner'=4] {'outer_0'}, dimensions={0}, use_global_device_ids=true | all-gather | bytes 163840 | tf_op jit(solution)/shard_map/all_gather | solution.py:30
  200.2 19.7 %all-gather.19.cloned.1.call-done = f32[64,8192]{1,0:T(8,128)} async-done(((f32[16,8192]{1,0:T(8,128)}), f32[64,8192]{1,0:T(8,128)}) %all-gather.19.cloned.1.call-update) | async-done | bytes 2097168 | tf_op jit(solution)/shard_map/all_gather | solution.py:30
  220.0 3.9 %fusion.23 = f32[16,8192]{1,0:T(8,128)} fusion(f32[64,8192]{1,0:T(8,128)} %all-gather.19.cloned.1.call-done, f32[16,8192]{1,0:T(8,128)S(1)} %copy-done.4, f32[16,8192]{1,0:T(8,128)S(1)} %get-tuple-element.378, f32[16,8192]{1,0:T(8,128)} %slice_add_fusion.9, f32[16,8192]{1,0:T(8,128)} %slice_add_fusion.5, f32[64,8192]{1,0:T(8,128)S(1)} %copy-done.3, ...), kind=kLoop, calls=%fused_computation.51 | loop fusion | flops 7602176 | bytes 8847374 | tf_op jit(solution)/shard_map/add | solution.py:95
  226.3 36.9 %while.27 = (s32[]{:T(128)}, f32[8,16,8192]{2,1,0:T(8,128)}, f32[8,16,16]{2,1,0:T(8,128)S(1)}, f32[8,16,8192]{2,1,0:T(8,128)}, f32[16,8192]{1,0:T(8,128)S(1)}, /*index=5*/f32[16,8192]{1,0:T(8,128)S(1)}, s32[]{:T(128)}) while((s32[]{:T(128)}, f32[8,16,8192]{2,1,0:T(8,128)}, f32[8,16,16]{2,1,0:T(8,128)S(1)}, f32[8,16,8192]{2,1,0:T(8,128)}, ...), condition=%wide.region_7.8_spmd, body=%wide.region_5.7_spmd.sunk | while | flops 8388610 | bytes 4197473 | solution.py:106
  263.3 4.1 %add.215 = f32[8,16,8192]{2,1,0:T(8,128)S(1)} add(f32[8,16,8192]{2,1,0:T(8,128)} %get-tuple-element.92, f32[8,16,8192]{2,1,0:T(8,128)} %get-tuple-element.96) | non-fusion elementwise | flops 1048576 | bytes 12582912 | tf_op jit(solution)/shard_map/add | solution.py:107
  268.7 5.2 %fusion.12 = bf16[128,8192]{1,0:T(8,128)(2,1)} fusion(bf16[128,8192]{1,0:T(8,128)(2,1)S(1)} %copy-done.5, f32[8,16,8192]{2,1,0:T(8,128)S(1)} %add.215, f32[8192]{0:T(1024)S(1)} %copy-done.21, f32[131,8192]{1,0:T(8,128)S(1)} %bitcast.81, f32[8192]{0:T(1024)S(1)} %bitcast.101, f32[8192]{0:T(1024)S(1)} %bitcast.103, f32[8192]{0:T(1024)S(1)} %bitcast.99, ...), kind=kLoop, calls=%fused_computation.33 | loop fusion | flops 24117248 | bytes 25362432 | tf_op jit(solution)/shard_map/convert_element_type | solution.py:108
  (190 shorter events, 97.8 us)
Async XLA Ops:
  6.5 11.0 %copy-start.17 = (f32[8192]{0:T(1024)S(1)}, f32[8192]{0:T(1024)}, u32[]{:S(2)}) copy-start(f32[8192]{0:T(1024)} %param.16) | copy-start | bytes 98308
  6.5 130.3 %all-gather.13.cloned.1.call-start = ((), (), s32[]{:S(2)}) async-start(), calls=%async_computation | async-start | bytes 2621440 | tf_op jit(solution)/shard_map/all_gather | solution.py:30
  7.5 7.7 %collective-permute-start = (bf16[3,8192]{1,0:T(4,128)(2,1)S(1)}, bf16[3,8192]{1,0:T(4,128)(2,1)S(1)}, u32[]{:S(2)}, u32[]{:S(2)}) collective-permute-start(bf16[3,8192]{1,0:T(4,128)(2,1)S(1)} %slice.128), channel_id=1, source_target_pairs={{0,1},{1,2},{2,3},{3,4},{4,5},{5,6},{6,7},{7,8},{8,9},{9,10},{10,1... | collective-permute-start | bytes 147464 | tf_op jit(solution)/shard_map/ppermute | solution.py:16
  12.7 7.6 %copy-start.8 = (f32[1,8192]{1,0:T(1,128)}, f32[1,8192]{1,0:T(1,128)S(1)}, u32[]{:S(2)}) copy-start(f32[1,8192]{1,0:T(1,128)S(1)} %get-tuple-element.201) | copy-start | bytes 98308
  12.7 7.6 %copy-start.10 = (f32[1,8192]{1,0:T(1,128)}, f32[1,8192]{1,0:T(1,128)S(1)}, u32[]{:S(2)}) copy-start(f32[1,8192]{1,0:T(1,128)S(1)} %get-tuple-element.202) | copy-start | bytes 98308
  12.7 7.6 %copy-start.12 = (f32[1,8192]{1,0:T(1,128)}, f32[1,8192]{1,0:T(1,128)S(1)}, u32[]{:S(2)}) copy-start(f32[1,8192]{1,0:T(1,128)S(1)} %get-tuple-element.203) | copy-start | bytes 98308
  12.8 7.6 %copy-start.14 = (f32[1,8192]{1,0:T(1,128)}, f32[1,8192]{1,0:T(1,128)S(1)}, u32[]{:S(2)}) copy-start(f32[1,8192]{1,0:T(1,128)S(1)} %get-tuple-element.204) | copy-start | bytes 98308
  15.2 5.2 %slice-start.2 = ((s8[4718592]{0:T(1024)(128)(4,1)}), s8[4194304]{0:T(1024)(128)(4,1)S(1)}, s32[]{:S(2)}) async-start(s8[4718592]{0:T(1024)(128)(4,1)} %bitcast.82), calls=%async_computation.6 | async-start | bytes 8388608
  30.8 4.8 %copy-start.1 = (f32[16,8192]{1,0:T(8,128)S(1)}, f32[16,8192]{1,0:T(8,128)}, u32[]{:S(2)}) copy-start(f32[16,8192]{1,0:T(8,128)} %param.20) | copy-start | bytes 1572868
  104.2 47.7 %all-gather.15.cloned.1.call-start = ((), (), s32[]{:S(2)}) async-start(), calls=%async_computation.1 | async-start | bytes 1572864 | tf_op jit(solution)/shard_map/all_gather | solution.py:30
  139.5 80.5 %copy-start.3 = (f32[64,8192]{1,0:T(8,128)S(1)}, f32[64,8192]{1,0:T(8,128)}, u32[]{:S(2)}) copy-start(f32[64,8192]{1,0:T(8,128)} %all-gather.13.cloned.1.call-done) | copy-start | bytes 6291460
  139.5 80.5 %copy-start.4 = (f32[16,8192]{1,0:T(8,128)S(1)}, f32[16,8192]{1,0:T(8,128)}, u32[]{:S(2)}) copy-start(f32[16,8192]{1,0:T(8,128)} %slice_add_fusion.11) | copy-start | bytes 1572868
  139.5 46.5 %all-gather.17.cloned.1.call-start = ((), (), s32[]{:S(2)}) async-start(), calls=%async_computation.2 | async-start | bytes 2621440 | tf_op jit(solution)/shard_map/all_gather | solution.py:30
  154.1 65.9 %all-gather.19.cloned.1.call-start = ((), (), s32[]{:S(2)}) async-start(), calls=%async_computation.3 | async-start | bytes 2621440 | tf_op jit(solution)/shard_map/all_gather | solution.py:30
  156.4 63.5 %copy-start.7 = (f32[1,1,8192]{2,1,0:T(1,128)S(1)}, f32[1,1,8192]{2,1,0:T(1,128)}, u32[]{:S(2)}) copy-start(f32[1,1,8192]{2,1,0:T(1,128)} %get-tuple-element.193) | copy-start | bytes 98308
  156.5 63.5 %copy-start.19 = (f32[1,8192]{1,0:T(1,128)S(1)}, f32[1,8192]{1,0:T(1,128)}, u32[]{:S(2)}) copy-start(f32[1,8192]{1,0:T(1,128)} %get-tuple-element.177) | copy-start | bytes 98308
  156.5 63.5 %copy-start.20 = (f32[1,8192]{1,0:T(1,128)S(1)}, f32[1,8192]{1,0:T(1,128)}, u32[]{:S(2)}) copy-start(f32[1,8192]{1,0:T(1,128)} %get-tuple-element.208) | copy-start | bytes 98308
  263.2 5.4 %copy-start.5 = (bf16[128,8192]{1,0:T(8,128)(2,1)S(1)}, bf16[128,8192]{1,0:T(8,128)(2,1)}, u32[]{:S(2)}) copy-start(bf16[128,8192]{1,0:T(8,128)(2,1)} %param.14) | copy-start | bytes 6291460
  263.2 5.4 %copy-start.9 = (f32[1,8192]{1,0:T(1,128)S(1)}, f32[1,8192]{1,0:T(1,128)}, u32[]{:S(2)}) copy-start(f32[1,8192]{1,0:T(1,128)} %copy-done.8) | copy-start | bytes 98308
  263.2 5.4 %copy-start.11 = (f32[1,8192]{1,0:T(1,128)S(1)}, f32[1,8192]{1,0:T(1,128)}, u32[]{:S(2)}) copy-start(f32[1,8192]{1,0:T(1,128)} %copy-done.10) | copy-start | bytes 98308
  263.2 5.4 %copy-start.13 = (f32[1,8192]{1,0:T(1,128)S(1)}, f32[1,8192]{1,0:T(1,128)}, u32[]{:S(2)}) copy-start(f32[1,8192]{1,0:T(1,128)} %copy-done.12) | copy-start | bytes 98308
  263.2 5.4 %copy-start.15 = (f32[1,8192]{1,0:T(1,128)S(1)}, f32[1,8192]{1,0:T(1,128)}, u32[]{:S(2)}) copy-start(f32[1,8192]{1,0:T(1,128)} %copy-done.14) | copy-start | bytes 98308
  263.3 5.4 %copy-start.18 = (f32[8192]{0:T(1024)S(1)}, f32[8192]{0:T(1024)}, u32[]{:S(2)}) copy-start(f32[8192]{0:T(1024)} %param.16) | copy-start | bytes 98308
  263.3 5.4 %copy-start.21 = (f32[8192]{0:T(1024)S(1)}, f32[8192]{0:T(1024)}, u32[]{:S(2)}) copy-start(f32[8192]{0:T(1024)} %param.21) | copy-start | bytes 98308
  (8 other events, 20.4 us)
Sparse Core Ops, SparseCore 0:
  104.3 32.4 all-gather.12
  139.6 12.1 all-gather.14
  154.2 31.7 all-gather.16
  188.9 31.0 all-gather.18
where the time goes:
time: 282 us; the launch traced here: 280 us
  other arithmetic  110 us (39%)
  waiting for transfers between devices  71.2 us (25%)
  local copies, waits for them, and re-layouts  37.2 us (13%)
  blocking collectives  33.4 us (12%)
  between operations  13.5 us (5%)
  matrix products  10.1 us (4%)
  starting transfers between devices  4.08 us (1%)
    all_gather x4, waiting for transfers between devices, prefix_by_axis(): pieces = jax.tree.map(lambda part: lax.all_gather(part, axis), running)  68.7 us
    another operation x8, other arithmetic, block_step(): running = jnp.cumsum(weighted, axis=0)  36.6 us
    all_gather x4, blocking collectives, prefix_by_axis(): pieces = jax.tree.map(lambda part: lax.all_gather(part, axis), running)  33.4 us
    reduce_sum x8, other arithmetic, correction(): return jnp.sum(c_blk[:, :, None] * faded, axis=1)  21.2 us
    add x4, other arithmetic, combine(): jnp.exp(-later[0][None, :] * decay_rates) * earlier[1] + later[1]  11.4 us
    dynamic_update_slice x8, other arithmetic, local(): lax.scan(block_step, start, (dt_blocks, in_blocks, b_blocks, c_blocks))  8.78 us
    mul x16, local copies, waits for them, and re-layouts, block_step(): weighted = jnp.exp(growth) * b_blk[:, :, None] * in_blk[:, None, :]  8.74 us
    dot_general x1, matrix products, local(): jnp.dot(dt_low, dt_proj, preferred_element_type=jnp.float32)  8.7 us
  transfers between devices with their start and end apart: 5, of which 5 were waited for; matrix products, arithmetic and copies ran while one was open for 2% of the time, Pallas kernels for 0%

commit v1 on v0

v1 whole, which is shorter than its diff:
```python
import functools
import math

import jax
import jax.numpy as jnp
from jax import lax
from jax.experimental import pallas as pl
from jax.experimental.pallas import tpu as pltpu
from jax.sharding import PartitionSpec as P

f32, bf16 = jnp.float32, jnp.bfloat16
MESH = pl.DeviceIdType.MESH
LOG2E = math.log2(math.e)
LN2 = math.log(2.0)
DT_CEILING = 0.25

T = 128
E = 8192
N = 16
R = 256
KW = 4
LANES = 128
J = 8
GW = J * LANES
G = E // GW
ROWS = T * J
AGG = G * N + G


def silu(v):
    d = 1.0 + jnp.exp2(v * -LOG2E)
    r = pl.reciprocal(d, approx=True)
    r = r * (2.0 - d * r)
    return v * r


def softplus_clipped(v):
    z = jnp.exp2(jnp.minimum(v, 0.0) * LOG2E)
    small = z * (1.0 - z * (0.5 - z * (1.0 / 3.0 - 0.25 * z)))
    big = jnp.log2(1.0 + z) * LN2
    return jnp.minimum(jnp.where(z < 0.03, small, big), DT_CEILING)


def split3(v):
    hi = v.astype(bf16).astype(f32)
    mid = (v - hi).astype(bf16).astype(f32)
    lo = (v - hi - mid).astype(bf16).astype(f32)
    return hi, mid, lo


def scan_kernel(x_hbm, prior_ref, cw_ref, cb_ref, xp_hbm, dp_hbm, db_ref, a_ref,
                y_hbm, c_hbm, u_hbm, cs_hbm, agg_ref,
                x_v, xp_v, dp_v, pad_v, u_v, bs_v, cs_v, ach_v, proj_v, dch_v, ich_v, ych_v, cch_v,
                in_sem, out_sem):
    def x_copy(g):
        return pltpu.make_async_copy(x_hbm.at[:, pl.ds(g * GW, GW)], x_v.at[g], in_sem.at[0, g])

    def xp_copy(g):
        return pltpu.make_async_copy(xp_hbm.at[pl.ds(g * GW, GW), :], xp_v.at[pl.ds(g * GW, GW), :], in_sem.at[1, g])

    def dp_copy(g):
        return pltpu.make_async_copy(dp_hbm.at[:, pl.ds(g * GW, GW)], dp_v.at[g], in_sem.at[2, g])

    for g in range(G):
        x_copy(g).start()
        xp_copy(g).start()
    for g in range(G):
        dp_copy(g).start()

    for q in range(E // LANES):
        g, j = q // J, q % J
        ach_v[g, pl.ds(j, N, stride=J), :] = a_ref[:, q * LANES:(q + 1) * LANES] * -LOG2E

    proj_v[...] = jnp.zeros_like(proj_v)

    def conv_group(g, _):
        off = pl.multiple_of(g * GW, GW)
        x_copy(g).wait()
        pad_v[0:8, :] = prior_ref[:, pl.ds(off, GW)].astype(f32)
        for s in range(0, GW, 256):
            pad_v[8:8 + T, s:s + 256] = x_v[g, :, s:s + 256].astype(f32)
        for s in range(0, GW, LANES):
            w = cw_ref[:, pl.ds(off + s, LANES)]
            acc = cb_ref[:, pl.ds(off + s, LANES)]
            for k in range(KW):
                acc = acc + w[k:k + 1] * pad_v[8 - (KW - 1) + k:8 - (KW - 1) + k + T, s:s + LANES]
            u_v[g, :, s:s + LANES] = silu(acc).astype(bf16)
        xp_copy(g).wait()
        proj_v[...] += jnp.dot(u_v[g], xp_v[pl.ds(off, GW), :], preferred_element_type=f32)
        pltpu.make_async_copy(u_v.at[g], u_hbm.at[g], out_sem.at[2, g]).start()
        return 0

    lax.fori_loop(0, G, conv_group, 0)

    row = lax.broadcasted_iota(jnp.int32, (256, 16), 0)
    col = lax.broadcasted_iota(jnp.int32, (256, 16), 1)
    repeat = (row // N == col).astype(bf16)
    row = lax.broadcasted_iota(jnp.int32, (256, 96), 0)
    col = lax.broadcasted_iota(jnp.int32, (256, 96), 1)
    own = row % N == col % N
    row = lax.broadcasted_iota(jnp.int32, (96, 256), 0)
    col = lax.broadcasted_iota(jnp.int32, (96, 256), 1)
    gather = (row // 48 == col // LANES).astype(bf16)

    def spread(k, _):
        r = pl.multiple_of(k * 16, 16)
        b = proj_v[pl.ds(r, 16), R:R + N]
        c = proj_v[pl.ds(r, 16), R + N:R + 2 * N]
        parts = jnp.concatenate([*split3(b), *split3(c)], axis=1).astype(bf16)
        wide = jnp.dot(repeat, parts, preferred_element_type=f32)
        wide = jnp.where(own, wide, 0.0).astype(bf16)
        full = jnp.dot(wide, gather, preferred_element_type=f32)
        r = pl.multiple_of(k * 256, 256)
        bs_v[pl.ds(r, 256), :] = full[:, :LANES]
        cs_v[pl.ds(r, 256), :] = full[:, LANES:]
        return 0

    lax.fori_loop(0, T // 16, spread, 0)
    cs_copy = pltpu.make_async_copy(cs_v, cs_hbm, out_sem.at[3, 0])
    cs_copy.start()

    def group(g, _):
        off = pl.multiple_of(g * GW, GW)
        dp_copy(g).wait()
        dt_low = proj_v[:, 0:R].astype(bf16)
        for s in range(0, GW, 256):
            v = jnp.dot(dt_low, dp_v[g, :, s:s + 256], preferred_element_type=f32)
            d = softplus_clipped(v + db_ref[:, pl.ds(off + s, 256)])
            i = d * u_v[g, :, s:s + 256].astype(f32)
            for h in range(2):
                j = s // LANES + h
                dch_v[pl.ds(j, T, stride=J), :] = d[:, h * LANES:(h + 1) * LANES]
                ich_v[pl.ds(j, T, stride=J), :] = i[:, h * LANES:(h + 1) * LANES]

        def steps(k, carry):
            h, cum = list(carry[0]), carry[1]
            for tt in range(8):
                t = k * 8 + tt
                r = pl.multiple_of(t * J, J)
                d = dch_v[pl.ds(r, J), :]
                i = ich_v[pl.ds(r, J), :]
                cum = cum + d
                cch_v[g, pl.ds(r, J), :] = cum
                ys = []
                for n in range(N):
                    e = jnp.exp2(d * ach_v[g, n * J:(n + 1) * J, :])
                    b = bs_v[pl.ds(t * N + n, J, stride=0), :]
                    c = cs_v[pl.ds(t * N + n, J, stride=0), :]
                    h[n] = e * h[n] + b * i
                    ys.append(c * h[n])
                    if n % 4 == 3:
                        y4 = (ys[0] + ys[1]) + (ys[2] + ys[3])
                        y = y4 if n == 3 else y + y4
                        ys = []
                ych_v[g, pl.ds(r, J), :] = y
            return tuple(h), cum

        zero = jnp.zeros((J, LANES), f32)
        h, cum = lax.fori_loop(0, T // 8, steps, ((zero,) * N, zero))
        for n in range(N):
            agg_ref[pl.ds(g * N + n, J, stride=AGG), :] = h[n]
        agg_ref[pl.ds(G * N + g, J, stride=AGG), :] = cum
        pltpu.make_async_copy(ych_v.at[g], y_hbm.at[g], out_sem.at[0, g]).start()
        pltpu.make_async_copy(cch_v.at[g], c_hbm.at[g], out_sem.at[1, g]).start()
        return 0

    lax.fori_loop(0, G, group, 0)
    cs_copy.wait()
    for g in range(G):
        pltpu.make_async_copy(ych_v.at[g], y_hbm.at[g], out_sem.at[0, g]).wait()
        pltpu.make_async_copy(cch_v.at[g], c_hbm.at[g], out_sem.at[1, g]).wait()
        pltpu.make_async_copy(u_v.at[g], u_hbm.at[g], out_sem.at[2, g]).wait()


def exchange_kernel(agg_ref, a_ref, carry_ref, got_v, total_v, ys_v, zs_v, in_v, back_v,
                    send1, recv1, sendy, recvy, sendz, recvz, send4, recv4, own_sem):
    outer, x = lax.axis_index("outer"), lax.axis_index("inner")
    core, y, z = outer % 2, (outer // 2) % 4, outer // 8
    me = core * 4 + x

    def member(m):
        return ((z * 4 + y) * 2 + m // 4, m % 4)

    def at_y(v):
        return ((z * 4 + v) * 2 + core, x)

    def at_z(v):
        return ((v * 4 + y) * 2 + core, x)

    barrier = pltpu.get_barrier_semaphore()
    for r in range(1, 8):
        pl.semaphore_signal(barrier, inc=1, device_id=member((me + r) % 8), device_id_type=MESH)
    for r in range(1, 4):
        pl.semaphore_signal(barrier, inc=1, device_id=at_y((y + r) % 4), device_id_type=MESH)
        pl.semaphore_signal(barrier, inc=1, device_id=at_z((z + r) % 4), device_id_type=MESH)
    pl.semaphore_wait(barrier, 13)

    own = pltpu.make_async_copy(agg_ref.at[me], got_v.at[me], own_sem)
    own.start()
    first = []
    for r in range(1, 8):
        to = (me + r) % 8
        cp = pltpu.make_async_remote_copy(
            src_ref=agg_ref.at[to], dst_ref=got_v.at[me], send_sem=send1.at[r], recv_sem=recv1.at[r],
            device_id=member(to), device_id_type=MESH)
        cp.start()
        first.append(cp)
    own.wait()
    for cp in first:
        cp.wait()

    def rates(g):
        return a_ref[:, pl.ds(pl.multiple_of(g * GW + me * LANES, LANES), LANES)] * -LOG2E

    def advance(state, block, g):
        d = block[pl.ds(G * N + g, N, stride=0), :]
        return jnp.exp2(d * rates(g)) * state + block[pl.ds(g * N, N), :]

    dsum = got_v[0, G * N:AGG, :]
    for k in range(1, 8):
        dsum = dsum + got_v[k, G * N:AGG, :]
    total_v[G * N:AGG, :] = dsum
    for g in range(G):
        s = got_v[0, g * N:(g + 1) * N, :]
        for k in range(1, 8):
            s = advance(s, got_v.at[k], g)
        total_v[g * N:(g + 1) * N, :] = s

    def along(source, slots, here, place, send, recv):
        copies = []
        for r in range(1, 4):
            to = (here + r) % 4
            cp = pltpu.make_async_remote_copy(
                src_ref=source, dst_ref=slots.at[here], send_sem=send.at[r], recv_sem=recv.at[r],
                device_id=place(to), device_id_type=MESH)
            cp.start()
            copies.append(cp)
        slots[pl.ds(here, 1)] = source[...][None]
        for cp in copies:
            cp.wait()

    along(total_v, ys_v, y, at_y, sendy, recvy)
    dsum = ys_v[0, G * N:AGG, :]
    dpre = jnp.where(y > 0, dsum, 0.0)
    for k in range(1, 4):
        dpre = dpre + jnp.where(y > k, ys_v[k, G * N:AGG, :], 0.0)
        dsum = dsum + ys_v[k, G * N:AGG, :]
    in_v[G * N:AGG, :] = dpre
    total_v[G * N:AGG, :] = dsum
    for g in range(G):
        s = ys_v[0, g * N:(g + 1) * N, :]
        pre = jnp.where(y > 0, s, 0.0)
        for k in range(1, 4):
            s = advance(s, ys_v.at[k], g)
            pre = jnp.where(y > k, s, pre)
        in_v[g * N:(g + 1) * N, :] = pre
        total_v[g * N:(g + 1) * N, :] = s

    along(total_v, zs_v, z, at_z, sendz, recvz)
    for g in range(G):
        s = zs_v[0, g * N:(g + 1) * N, :]
        pre = jnp.where(z > 0, s, 0.0)
        for k in range(1, 3):
            s = advance(s, zs_v.at[k], g)
            pre = jnp.where(z > k, s, pre)
        s = advance(pre, in_v, g)
        for k in range(8):
            back_v[k, g * N:(g + 1) * N, :] = s
            if k < 7:
                s = advance(s, got_v.at[k], g)

    own = pltpu.make_async_copy(back_v.at[me], carry_ref.at[me], own_sem)
    own.start()
    last = []
    for r in range(1, 8):
        to = (me + r) % 8
        cp = pltpu.make_async_remote_copy(
            src_ref=back_v.at[to], dst_ref=carry_ref.at[me], send_sem=send4.at[r], recv_sem=recv4.at[r],
            device_id=member(to), device_id_type=MESH)
        cp.start()
        last.append(cp)
    own.wait()
    for cp in last:
        cp.wait()


def finish_kernel(y_hbm, c_hbm, u_hbm, cs_hbm, gate_hbm, carry_ref, a_ref, skip_ref,
                  out_hbm, y_v, c_v, u_v, cs_v, gate_v, ach_v, hch_v, out_v, in_sem, out_sem):
    def copies(g):
        cols = pl.ds(pl.multiple_of(g * GW, GW), GW)
        return (pltpu.make_async_copy(y_hbm.at[g], y_v.at[g], in_sem.at[0, g]),
                pltpu.make_async_copy(c_hbm.at[g], c_v.at[g], in_sem.at[1, g]),
                pltpu.make_async_copy(u_hbm.at[g], u_v.at[g], in_sem.at[2, g]),
                pltpu.make_async_copy(gate_hbm.at[:, cols], gate_v.at[g], in_sem.at[3, g]))

    def out_copy(g):
        cols = pl.ds(pl.multiple_of(g * GW, GW), GW)
        return pltpu.make_async_copy(out_v.at[g], out_hbm.at[:, cols], out_sem.at[g])

    cs_copy = pltpu.make_async_copy(cs_hbm, cs_v, in_sem.at[4, 0])
    cs_copy.start()
    for g in range(G):
        for cp in copies(g):
            cp.start()
    for q in range(E // LANES):
        g, j = q // J, q % J
        ach_v[g, pl.ds(j, N, stride=J), :] = a_ref[:, q * LANES:(q + 1) * LANES] * -LOG2E
    cs_copy.wait()

    def group(g, _):
        off = pl.multiple_of(g * GW, GW)
        for cp in copies(g):
            cp.wait()
        for n in range(N):
            hch_v[n * J:(n + 1) * J, :] = carry_ref[pl.ds(g * N + n, J, stride=G * N), :]

        def steps(k, _):
            for tt in range(8):
                t = k * 8 + tt
                r = pl.multiple_of(t * J, J)
                cum = c_v[g, pl.ds(r, J), :]
                y = y_v[g, pl.ds(r, J), :]
                for n4 in range(0, N, 4):
                    part = []
                    for n in range(n4, n4 + 4):
                        e = jnp.exp2(cum * ach_v[g, n * J:(n + 1) * J, :])
                        c = cs_v[pl.ds(t * N + n, J, stride=0), :]
                        part.append(c * (e * hch_v[n * J:(n + 1) * J, :]))
                    y = y + ((part[0] + part[1]) + (part[2] + part[3]))
                y_v[g, pl.ds(r, J), :] = y
            return 0

        lax.fori_loop(0, T // 8, steps, 0)
        for j in range(J):
            cols = slice(j * LANES, (j + 1) * LANES)
            y = y_v[g, pl.ds(j, T, stride=J), :]
            y = y + skip_ref[:, pl.ds(off + j * LANES, LANES)] * u_v[g, :, cols].astype(f32)
            out_v[g, :, cols] = (y * silu(gate_v[g, :, cols].astype(f32))).astype(bf16)
        out_copy(g).start()
        return 0

    lax.fori_loop(0, G, group, 0)
    for g in range(G):
        out_copy(g).wait()


ANY = pl.BlockSpec(memory_space=pl.ANY)
VMEM = pl.BlockSpec(memory_space=pltpu.VMEM)
VMEM_BYTES = 56 * 2**20


def local(x_in, gate_in, conv_weight, conv_bias, x_proj, dt_proj, dt_bias, decay_rates, skip_gain):
    sds = jax.ShapeDtypeStruct
    devices = lax.axis_size("outer") * lax.axis_size("inner")
    prior = lax.ppermute(x_in[T - 8:], ("outer", "inner"), [(s, s + 1) for s in range(devices - 1)])
    y, c, u, cs, agg = pl.pallas_call(
        scan_kernel,
        name="local_scan",
        out_shape=[sds((G, ROWS, LANES), f32), sds((G, ROWS, LANES), f32), sds((G, T, GW), bf16),
                   sds((T * N, LANES), f32), sds((J * AGG, LANES), f32)],
        in_specs=[ANY, VMEM, VMEM, VMEM, ANY, ANY, VMEM, VMEM],
        out_specs=[ANY, ANY, ANY, ANY, VMEM],
        scratch_shapes=[
            pltpu.VMEM((G, T, GW), bf16), pltpu.VMEM((E, R + 2 * N), bf16), pltpu.VMEM((G, R, GW), bf16),
            pltpu.VMEM((T + 8, GW), f32), pltpu.VMEM((G, T, GW), bf16),
            pltpu.VMEM((T * N, LANES), f32), pltpu.VMEM((T * N, LANES), f32),
            pltpu.VMEM((G, N * J, LANES), f32), pltpu.VMEM((T, R + 2 * N), f32),
            pltpu.VMEM((ROWS, LANES), f32), pltpu.VMEM((ROWS, LANES), f32),
            pltpu.VMEM((G, ROWS, LANES), f32), pltpu.VMEM((G, ROWS, LANES), f32),
            pltpu.SemaphoreType.DMA((3, G)), pltpu.SemaphoreType.DMA((4, G))],
        compiler_params=pltpu.CompilerParams(vmem_limit_bytes=VMEM_BYTES),
    )(x_in, prior, conv_weight, conv_bias.reshape(1, E), x_proj, dt_proj, dt_bias.reshape(1, E), decay_rates)

    carry = pl.pallas_call(
        exchange_kernel,
        name="exchange",
        out_shape=sds((J, G * N, LANES), f32),
        in_specs=[VMEM, VMEM],
        out_specs=VMEM,
        scratch_shapes=[
            pltpu.VMEM((8, AGG, LANES), f32), pltpu.VMEM((AGG, LANES), f32),
            pltpu.VMEM((4, AGG, LANES), f32), pltpu.VMEM((4, AGG, LANES), f32), pltpu.VMEM((AGG, LANES), f32),
            pltpu.VMEM((8, G * N, LANES), f32),
            pltpu.SemaphoreType.DMA((8,)), pltpu.SemaphoreType.DMA((8,)),
            pltpu.SemaphoreType.DMA((4,)), pltpu.SemaphoreType.DMA((4,)),
            pltpu.SemaphoreType.DMA((4,)), pltpu.SemaphoreType.DMA((4,)),
            pltpu.SemaphoreType.DMA((8,)), pltpu.SemaphoreType.DMA((8,)),
            pltpu.SemaphoreType.DMA],
        compiler_params=pltpu.CompilerParams(collective_id=0, has_side_effects=True, vmem_limit_bytes=32 * 2**20),
    )(agg.reshape(J, AGG, LANES), decay_rates)

    return pl.pallas_call(
        finish_kernel,
        name="finish",
        out_shape=sds((T, E), bf16),
        in_specs=[ANY, ANY, ANY, ANY, ANY, VMEM, VMEM, VMEM],
        out_specs=ANY,
        scratch_shapes=[
            pltpu.VMEM((G, ROWS, LANES), f32), pltpu.VMEM((G, ROWS, LANES), f32), pltpu.VMEM((G, T, GW), bf16),
            pltpu.VMEM((T * N, LANES), f32), pltpu.VMEM((G, T, GW), bf16),
            pltpu.VMEM((G, N * J, LANES), f32), pltpu.VMEM((N * J, LANES), f32), pltpu.VMEM((G, T, GW), bf16),
            pltpu.SemaphoreType.DMA((5, G)), pltpu.SemaphoreType.DMA((G,))],
        compiler_params=pltpu.CompilerParams(vmem_limit_bytes=VMEM_BYTES),
    )(y, c, u, cs, gate_in, carry.reshape(J * G * N, LANES), decay_rates, skip_gain.reshape(1, E))


def solution(mesh):
    tokens = P(("outer", "inner"), None)
    return jax.shard_map(
        local, mesh=mesh, in_specs=(tokens, tokens, P(), P(), P(), P(), P(), P(), P()),
        out_specs=tokens, check_vma=False)
```

time: 282 us -> 104 us (0.37)
  other arithmetic: 110 us -> 0 us
  Pallas kernels: 0 us -> 87.4 us
  waiting for transfers between devices: 71.2 us -> 0.01 us
  blocking collectives: 33.4 us -> 0 us
  local copies, waits for them, and re-layouts: 37.2 us -> 11.3 us
  between operations: 13.5 us -> 0.06 us
  matrix products: 10.1 us -> 0 us
    pallas_call x0 -> x3, Pallas kernels: none -> 87.4 us  [the longest x1 35.6 us: local(): pl.pallas_call(scan_kernel, name='local_scan', out_shape=[sds((G, ROWS, L...]
    all_gather x4 -> x0, waiting for transfers between devices: 68.7 us -> none  [prefix_by_axis(): pieces = jax.tree.map(lambda part: lax.all_gather(part, axis), running)]
    another operation x16 -> x0, other arithmetic: 40.3 us -> none  [the longest x8 36.6 us: block_step(): running = jnp.cumsum(weighted, axis=0)]
    all_gather x4 -> x0, blocking collectives: 33.4 us -> none  [prefix_by_axis(): pieces = jax.tree.map(lambda part: lax.all_gather(part, axis), running)]
    reduce_sum x8 -> x0, other arithmetic: 21.2 us -> none  [correction(): return jnp.sum(c_blk[:, :, None] * faded, axis=1)]
    add x15 -> x0, other arithmetic: 17.4 us -> none  [the longest x4 11.4 us: combine(): jnp.exp(-later[0][None, :] * decay_rates) * earlier[1] + later[1]]
    neg x11 -> x0, other arithmetic: 11.7 us -> none  [the longest x8 8.61 us: correction(): -cum_blk[:, None, :] * decay_rates[None, :, :]]
    convert_element_type x3 -> x0, other arithmetic: 10.2 us -> none  [the longest x1 5.16 us: local(): (y_full * jax.nn.silu(gate_in.astype(jnp.float32))).astype(jnp.bfloat16)]
  transfers between devices with their start and end apart: 5 -> 1, of which waited for: 5 -> 0; matrix products, arithmetic and copies ran while one was open for 2% -> 8% of each run, Pallas kernels for 0% -> 0%
where the time goes in v1:
time: 104 us; the launch traced here: 103 us
  Pallas kernels  87.4 us (84%)
  local copies, waits for them, and re-layouts  11.3 us (11%)
  starting transfers between devices  3.95 us (4%)
    pallas_call x1, Pallas kernels, local(): pl.pallas_call(scan_kernel, name='local_scan', out_shape=[sds((G, ROWS, L...  35.6 us
    pallas_call x1, Pallas kernels, local(): pl.pallas_call(exchange_kernel, name='exchange', out_shape=sds((J, G * N,...  32.7 us
    pallas_call x1, Pallas kernels, local(): pl.pallas_call(finish_kernel, name='finish', out_shape=sds((T, E), bf16),...  19.1 us
    unnamed x9, local copies, waits for them, and re-layouts  10.4 us
    ppermute x1, starting transfers between devices, local(): lax.ppermute(x_in[T - 8:], ('outer', 'inner'), [(s, s + 1) for s in range...  3.95 us
  transfers between devices with their start and end apart: 1, of which 0 were waited for; matrix products, arithmetic and copies ran while one was open for 8% of the time, Pallas kernels for 0%

profile of v1, /device:TPU:1, one launch (start us, length us, event | category | flops | bytes accessed | tf_op | source)
XLA Modules:
  0.0 102.7 jit_solution(5449868138008772138)
XLA Ops:
  0.0 0.9 slice.3
  0.9 3.9 %collective-permute-start = (bf16[8,8192]{1,0:T(8,128)(2,1)S(1)}, bf16[8,8192]{1,0:T(8,128)(2,1)S(1)}, u32[]{:S(2)}, u32[]{:S(2)}) collective-permute-start(bf16[8,8192]{1,0:T(8,128)(2,1)S(1)} %slice.3), channel_id=1, source_target_pairs={{0,1},{1,2},{2,3},{3,4},{4,5},{5,6},{6,7},{7,8},{8,9},{9,10},{10,1... | collective-permute-start | bytes 393224 | tf_op jit(solution)/shard_map/ppermute | solution.py:355
  4.9 7.9 %copy.10.xp_hbm = bf16[8192,288]{1,0:T(8,128)(2,1)} copy(bf16[8192,288]{0,1:T(8,128)(2,1)} %param.13) | data formatting | bytes 9437184 | tf_op args[4]
  12.8 0.0 collective-permute-done.prior_ref
  12.8 0.0 copy-start.3
  12.8 0.6 copy-done.3
  13.5 0.0 copy-start
  13.5 35.6 %local_scan.1 = (f32[8,1024,128]{2,1,0:T(8,128)}, f32[8,1024,128]{2,1,0:T(8,128)}, bf16[8,128,1024]{2,1,0:T(8,128)(2,1)}, f32[2048,128]{1,0:T(8,128)}, f32[1088,128]{1,0:T(8,128)}) custom-call(bf16[128,8192]{1,0:T(8,128)(2,1)} %x_hbm.1, bf16[8,8192]{1,0:T(8,128)(2,1)} %copy-done.3, f32[4,8192]{1,0:T(4,128)} %cw_ref.1, f32[1,8192]{1,0:T(1,128)} %bitcast.7, ...), custom_call_target="tpu_custom_call" | custom-call | tf_op jit(solution)/shard_map/local_scan/pallas_call | solution.py:356
  49.1 0.0 copy-done
  49.1 0.0 copy-start.2
  49.1 1.0 %copy-done.2 = f32[1088,128]{1,0:T(8,128)S(1)} copy-done((f32[1088,128]{1,0:T(8,128)S(1)}, f32[1088,128]{1,0:T(8,128)}, u32[]{:S(2)}) %copy-start.2) | copy-done | bytes 557080
  50.1 32.7 %exchange.1 = f32[8,128,128]{2,1,0:T(8,128)S(1)} custom-call(f32[8,136,128]{2,1,0:T(8,128)S(1)} %bitcast.6, f32[16,8192]{1,0:T(8,128)S(1)} %copy-done), custom_call_target="tpu_custom_call" | custom-call | tf_op jit(solution)/shard_map/exchange/pallas_call | solution.py:374
  82.8 0.0 copy-start.1
  82.8 0.8 copy-done.1
  83.6 19.1 %finish.1 = bf16[128,8192]{1,0:T(8,128)(2,1)} custom-call(f32[8,1024,128]{2,1,0:T(8,128)} %get-tuple-element.10.y_hbm, f32[8,1024,128]{2,1,0:T(8,128)} %get-tuple-element.11.c_hbm, bf16[8,128,1024]{2,1,0:T(8,128)(2,1)} %get-tuple-element.12.u_hbm, f32[2048,128]{1,0:T(8,128)} %get-tuple-element.13.cs_hbm, bf16[128,8192]{1,0:T(8,128)(2,1)} %gate_hbm.1, ...), custom_call_target="tpu_custom_call" | custom-call | tf_op jit(solution)/shard_map/finish/pallas_call | solution.py:392
Async XLA Ops:
  0.9 11.9 %collective-permute-start = (bf16[8,8192]{1,0:T(8,128)(2,1)S(1)}, bf16[8,8192]{1,0:T(8,128)(2,1)S(1)}, u32[]{:S(2)}, u32[]{:S(2)}) collective-permute-start(bf16[8,8192]{1,0:T(8,128)(2,1)S(1)} %slice.3), channel_id=1, source_target_pairs={{0,1},{1,2},{2,3},{3,4},{4,5},{5,6},{6,7},{7,8},{8,9},{9,10},{10,1... | collective-permute-start | bytes 393224 | tf_op jit(solution)/shard_map/ppermute | solution.py:355
  12.8 0.6 copy-start.3
  13.5 35.6 %copy-start = (f32[16,8192]{1,0:T(8,128)S(1)}, f32[16,8192]{1,0:T(8,128)}, u32[]{:S(2)}) copy-start(f32[16,8192]{1,0:T(8,128)} %a_ref.5) | copy-start | bytes 1572868
  49.1 1.1 %copy-start.2 = (f32[1088,128]{1,0:T(8,128)S(1)}, f32[1088,128]{1,0:T(8,128)}, u32[]{:S(2)}) copy-start(f32[1088,128]{1,0:T(8,128)} %get-tuple-element.14) | copy-start | bytes 1671172
  82.8 0.8 copy-start.1

commit v2 on v0

v2 whole, which is shorter than its diff:
```python
import math

import jax
import jax.numpy as jnp
from jax import lax
from jax.experimental import pallas as pl
from jax.experimental.pallas import tpu as pltpu
from jax.sharding import PartitionSpec as P

f32, bf16 = jnp.float32, jnp.bfloat16
MESH = pl.DeviceIdType.MESH
LOG2E = math.log2(math.e)
LN2 = math.log(2.0)
DT_CEILING = 0.25

T = 128
E = 8192
N = 16
R = 256
KW = 4
LANES = 128
J = 8
GW = J * LANES
G = E // GW
ROWS = T * J
C = G // 2
AGG = 40
HALO = 16


def silu(v):
    d = 1.0 + jnp.exp2(v * -LOG2E)
    r = pl.reciprocal(d, approx=True)
    r = r * (2.0 - d * r)
    return v * r


def softplus_clipped(v):
    z = jnp.exp2(jnp.minimum(v, 0.0) * LOG2E)
    small = z * (1.0 - z * (0.5 - z * (1.0 / 3.0 - 0.25 * z)))
    big = jnp.log2(1.0 + z) * LN2
    return jnp.minimum(jnp.where(z < 0.03, small, big), DT_CEILING)


def split3(v):
    hi = v.astype(bf16).astype(f32)
    mid = (v - hi).astype(bf16).astype(f32)
    lo = (v - hi - mid).astype(bf16).astype(f32)
    return hi, mid, lo


def kernel(x_hbm, gate_hbm, cw_hbm, cb_hbm, xp_hbm, dp_hbm, db_hbm, a_hbm, sk_hbm, out_hbm,
           x_v, gate_v, cw_v, cb_v, xp_v, dp_v, db_v, a_v, sk_v, halo_v, xch_v, wch_v, u_v, bs_v, cs_v, ach_v,
           proj_v, dch_v, ich_v, ych_v, cch_v, out_v,
           agg_v, got_v, total_v, ys_v, part_v, ytotal_v, zs_v, back_v, carry_v,
           in_sem, one_sem, out_sem, hsend, hrecv, send1, recv1, sendy, recvy, sendz, recvz, send4, recv4):
    outer, x = lax.axis_index("outer"), lax.axis_index("inner")
    core, y, z = outer % 2, (outer // 2) % 4, outer // 8
    me = core * 4 + x
    line = outer * 4 + x

    def in_copy(kind, g):
        cols = pl.ds(pl.multiple_of(g * GW, GW), GW)
        source, target = ((x_hbm, x_v), (xp_hbm, xp_v), (dp_hbm, dp_v), (gate_hbm, gate_v))[kind]
        return pltpu.make_async_copy(source.at[:, cols], target.at[g], in_sem.at[kind, g])

    ones = [pltpu.make_async_copy(s, t, one_sem.at[k]) for k, (s, t) in enumerate(
        ((cw_hbm, cw_v), (cb_hbm, cb_v), (a_hbm, a_v), (db_hbm, db_v), (sk_hbm, sk_v)))]
    for cp in ones[:2]:
        cp.start()
    for g in range(G):
        in_copy(0, g).start()
        in_copy(1, g).start()
    for cp in ones[2:]:
        cp.start()
    for g in range(G):
        in_copy(2, g).start()
    for g in range(G):
        in_copy(3, g).start()

    def at_line(v):
        return (v // 4, v % 4)

    def member(m):
        return ((z * 4 + y) * 2 + m // 4, m % 4)

    def at_y(v):
        return ((z * 4 + v) * 2 + core, x)

    def at_z(v):
        return ((v * 4 + y) * 2 + core, x)

    devices = lax.axis_size("outer") * lax.axis_size("inner")
    barrier = pltpu.get_barrier_semaphore()
    after, before = (line + 1) % devices, (line + devices - 1) % devices
    pl.semaphore_signal(barrier, inc=1, device_id=at_line(after), device_id_type=MESH)
    pl.semaphore_signal(barrier, inc=1, device_id=at_line(before), device_id_type=MESH)
    for r in range(1, 8):
        pl.semaphore_signal(barrier, inc=1, device_id=member((me + r) % 8), device_id_type=MESH)
    for r in range(1, 4):
        pl.semaphore_signal(barrier, inc=1, device_id=at_y((y + r) % 4), device_id_type=MESH)
        pl.semaphore_signal(barrier, inc=1, device_id=at_z((z + r) % 4), device_id_type=MESH)
    pl.semaphore_wait(barrier, 15)

    def halo_copy(g):
        cols = pl.ds(pl.multiple_of(g * GW, GW), GW)
        return pltpu.make_async_remote_copy(
            src_ref=x_hbm.at[pl.ds(T - HALO, HALO), cols], dst_ref=halo_v.at[g], send_sem=hsend.at[g],
            recv_sem=hrecv.at[g], device_id=at_line(after), device_id_type=MESH)

    for g in range(G):
        halo_copy(g).start()

    def rows(index, count):
        return pl.ds(pl.multiple_of(index * count, 8), count)

    def first_copy(c, r):
        to = (me + r) % 8
        return pltpu.make_async_remote_copy(
            src_ref=agg_v.at[rows(c * 8 + to, AGG), :], dst_ref=got_v.at[rows(c * 8 + me, AGG), :],
            send_sem=send1.at[c, r], recv_sem=recv1.at[c, r], device_id=member(to), device_id_type=MESH)

    def y_copy(c, r):
        return pltpu.make_async_remote_copy(
            src_ref=total_v.at[rows(c, AGG), :], dst_ref=ys_v.at[rows(c * 4 + y, AGG), :],
            send_sem=sendy.at[c, r], recv_sem=recvy.at[c, r], device_id=at_y((y + r) % 4), device_id_type=MESH)

    def z_copy(c, r):
        return pltpu.make_async_remote_copy(
            src_ref=ytotal_v.at[rows(c, AGG), :], dst_ref=zs_v.at[rows(c * 4 + z, AGG), :],
            send_sem=sendz.at[c, r], recv_sem=recvz.at[c, r], device_id=at_z((z + r) % 4), device_id_type=MESH)

    def last_copy(c, r):
        to = (me + r) % 8
        return pltpu.make_async_remote_copy(
            src_ref=back_v.at[rows(c * 8 + to, 2 * N), :], dst_ref=carry_v.at[rows(c * 8 + me, 2 * N), :],
            send_sem=send4.at[c, r], recv_sem=recv4.at[c, r], device_id=member(to), device_id_type=MESH)

    agg_v[...] = jnp.zeros_like(agg_v)
    total_v[...] = jnp.zeros_like(total_v)
    ytotal_v[...] = jnp.zeros_like(ytotal_v)
    proj_v[...] = jnp.zeros_like(proj_v)
    for cp in ones[:2]:
        cp.wait()
    for q in range(E // LANES):
        g, j, cols = q // J, q % J, slice(q * LANES, (q + 1) * LANES)
        wch_v[g, pl.ds(j, KW, stride=J), :] = cw_v[:, cols]
        wch_v[g, KW * J + j:KW * J + j + 1, :] = cb_v[:, cols]

    def conv_group(g, _):
        in_copy(0, g).wait()
        halo_copy(g).wait_recv()
        for j in range(J):
            cols = slice(j * LANES, (j + 1) * LANES)
            halo = halo_v[g, :, cols].astype(f32)
            xch_v[pl.ds(j, HALO, stride=J), :] = jnp.where(line > 0, halo, 0.0)
            xch_v[pl.ds(HALO * J + j, T, stride=J), :] = x_v[g, :, cols].astype(f32)

        def tokens(k, _):
            w = [wch_v[g, i * J:(i + 1) * J, :] for i in range(KW + 1)]
            for tt in range(16):
                r = pl.multiple_of((k * 16 + tt) * J, J)
                acc = w[KW]
                for i in range(KW):
                    acc = acc + w[i] * xch_v[pl.ds(r + (HALO - KW + 1 + i) * J, J), :]
                dch_v[pl.ds(r, J), :] = silu(acc)
            return 0

        lax.fori_loop(0, T // 16, tokens, 0)
        for j in range(J):
            u_v[g, :, j * LANES:(j + 1) * LANES] = dch_v[pl.ds(j, T, stride=J), :].astype(bf16)
        in_copy(1, g).wait()
        proj_v[...] += lax.dot_general(u_v[g], xp_v[g], (((1,), (1,)), ((), ())), preferred_element_type=f32)
        return 0

    lax.fori_loop(0, G, conv_group, 0)

    row = lax.broadcasted_iota(jnp.int32, (256, 16), 0)
    col = lax.broadcasted_iota(jnp.int32, (256, 16), 1)
    repeat = (row // N == col).astype(bf16)
    row = lax.broadcasted_iota(jnp.int32, (256, 96), 0)
    col = lax.broadcasted_iota(jnp.int32, (256, 96), 1)
    own = row % N == col % N
    row = lax.broadcasted_iota(jnp.int32, (96, 256), 0)
    col = lax.broadcasted_iota(jnp.int32, (96, 256), 1)
    gather = (row // 48 == col // LANES).astype(bf16)

    def spread(k, _):
        r = pl.multiple_of(k * 16, 16)
        b = proj_v[pl.ds(r, 16), R:R + N]
        c = proj_v[pl.ds(r, 16), R + N:R + 2 * N]
        parts = jnp.concatenate([*split3(b), *split3(c)], axis=1).astype(bf16)
        wide = jnp.dot(repeat, parts, preferred_element_type=f32)
        wide = jnp.where(own, wide, 0.0).astype(bf16)
        full = jnp.dot(wide, gather, preferred_element_type=f32)
        r = pl.multiple_of(k * 256, 256)
        bs_v[pl.ds(r, 256), :] = full[:, :LANES]
        cs_v[pl.ds(r, 256), :] = full[:, LANES:]
        return 0

    lax.fori_loop(0, T // 16, spread, 0)

    for cp in ones[2:]:
        cp.wait()
    for q in range(E // LANES):
        ach_v[q // J, pl.ds(q % J, N, stride=J), :] = a_v[:, q * LANES:(q + 1) * LANES] * -LOG2E

    def scan_group(g, c, half):
        off = pl.multiple_of(g * GW, GW)
        in_copy(2, g).wait()
        dt_low = proj_v[:, 0:R].astype(bf16)
        for s in range(0, GW, 256):
            v = jnp.dot(dt_low, dp_v[g, :, s:s + 256], preferred_element_type=f32)
            d = softplus_clipped(v + db_v[:, pl.ds(off + s, 256)])
            i = d * u_v[g, :, s:s + 256].astype(f32)
            for h in range(2):
                j = s // LANES + h
                dch_v[pl.ds(j, T, stride=J), :] = d[:, h * LANES:(h + 1) * LANES]
                ich_v[pl.ds(j, T, stride=J), :] = i[:, h * LANES:(h + 1) * LANES]

        def steps(k, carry):
            h, cum = list(carry[0]), carry[1]
            for tt in range(UNROLL):
                t = k * UNROLL + tt
                r = pl.multiple_of(t * J, J)
                d = dch_v[pl.ds(r, J), :]
                i = ich_v[pl.ds(r, J), :]
                cum = cum + d
                cch_v[g, pl.ds(r, J), :] = cum
                ys = []
                for n in range(N):
                    e = jnp.exp2(d * ach_v[g, n * J:(n + 1) * J, :])
                    b = bs_v[pl.ds(t * N + n, J, stride=0), :]
                    c_n = cs_v[pl.ds(t * N + n, J, stride=0), :]
                    h[n] = e * h[n] + b * i
                    ys.append(c_n * h[n])
                    if n % 4 == 3:
                        y4 = (ys[0] + ys[1]) + (ys[2] + ys[3])
                        y_t = y4 if n == 3 else y_t + y4
                        ys = []
                ych_v[g, pl.ds(r, J), :] = y_t
            return tuple(h), cum

        zero = jnp.zeros((J, LANES), f32)
        h, cum = lax.fori_loop(0, T // UNROLL, steps, ((zero,) * N, zero))
        for n in range(N):
            agg_v[pl.ds(c * (J * AGG) + half * N + n, J, stride=AGG), :] = h[n]
        agg_v[pl.ds(c * (J * AGG) + 2 * N + half, J, stride=AGG), :] = cum

    def rates(c, half):
        col = pl.multiple_of((c * 2 + half) * GW + me * LANES, LANES)
        return a_v[:, pl.ds(col, LANES)] * -LOG2E

    def advance(state, ref, slot, rate, half):
        d = ref[pl.ds(slot * AGG + 2 * N + half, N, stride=0), :]
        return jnp.exp2(d * rate) * state + ref[pl.ds(pl.multiple_of(slot * AGG + half * N, 8), N), :]

    def dsums(ref, slot):
        return ref[pl.ds(pl.multiple_of(slot * AGG + 2 * N, 8), 8), :]

    def put(ref, slot, row, count, value):
        ref[pl.ds(pl.multiple_of(slot * AGG + row, 8), count), :] = value

    def send_first(c):
        got_v[rows(c * 8 + me, AGG), :] = agg_v[rows(c * 8 + me, AGG), :]
        for r in range(1, 8):
            first_copy(c, r).start()

    def after_first(c):
        for r in range(1, 8):
            first_copy(c, r).wait_recv()
        d = dsums(got_v, c * 8)
        for k in range(1, 8):
            d = d + dsums(got_v, c * 8 + k)
        put(total_v, c, 2 * N, 8, d)
        put(ys_v, c * 4 + y, 2 * N, 8, d)
        for half in range(2):
            rate = rates(c, half)
            s = jnp.zeros((N, LANES), f32)
            for k in range(8):
                s = advance(s, got_v, c * 8 + k, rate, half)
            put(total_v, c, half * N, N, s)
            put(ys_v, c * 4 + y, half * N, N, s)
        for r in range(1, 4):
            y_copy(c, r).start()

    def after_y(c):
        for r in range(1, 4):
            y_copy(c, r).wait_recv()
        d = dsums(ys_v, c * 4)
        pre = jnp.where(y > 0, d, 0.0)
        for k in range(1, 4):
            now = dsums(ys_v, c * 4 + k)
            d = d + now
            pre = pre + jnp.where(y > k, now, 0.0)
        put(part_v, c, 2 * N, 8, pre)
        put(ytotal_v, c, 2 * N, 8, d)
        put(zs_v, c * 4 + z, 2 * N, 8, d)
        for half in range(2):
            rate = rates(c, half)
            s = jnp.zeros((N, LANES), f32)
            pre = s
            for k in range(4):
                s = advance(s, ys_v, c * 4 + k, rate, half)
                pre = jnp.where(y > k, s, pre)
            put(part_v, c, half * N, N, pre)
            put(ytotal_v, c, half * N, N, s)
            put(zs_v, c * 4 + z, half * N, N, s)
        for r in range(1, 4):
            z_copy(c, r).start()

    def after_z(c):
        for r in range(1, 4):
            z_copy(c, r).wait_recv()
        for half in range(2):
            rate = rates(c, half)
            s = jnp.zeros((N, LANES), f32)
            pre = s
            for k in range(3):
                s = advance(s, zs_v, c * 4 + k, rate, half)
                pre = jnp.where(z > k, s, pre)
            s = advance(pre, part_v, c, rate, half)
            for k in range(8):
                back_v[pl.ds(pl.multiple_of((c * 8 + k) * 2 * N + half * N, 8), N), :] = s
                if k < 7:
                    s = advance(s, got_v, c * 8 + k, rate, half)
        carry_v[rows(c * 8 + me, 2 * N), :] = back_v[rows(c * 8 + me, 2 * N), :]
        for r in range(1, 8):
            last_copy(c, r).start()

    def first_half(p, _):
        scan_group(2 * p, p, 0)
        pl.when(p >= 1)(lambda: after_first(p - 1))
        pl.when(p >= 2)(lambda: after_y(p - 2))
        pl.when(p >= 3)(lambda: after_z(p - 3))
        scan_group(2 * p + 1, p, 1)
        send_first(p)
        return 0

    lax.fori_loop(0, C, first_half, 0)

    def out_copy(g):
        cols = pl.ds(pl.multiple_of(g * GW, GW), GW)
        return pltpu.make_async_copy(out_v.at[g], out_hbm.at[:, cols], out_sem.at[g])

    def finish_group(g, c, half):
        off = pl.multiple_of(g * GW, GW)

        def steps(k, _):
            for tt in range(UNROLL2):
                t = k * UNROLL2 + tt
                r = pl.multiple_of(t * J, J)
                cum = cch_v[g, pl.ds(r, J), :]
                y_t = ych_v[g, pl.ds(r, J), :]
                for n4 in range(0, N, 4):
                    part = []
                    for n in range(n4, n4 + 4):
                        e = jnp.exp2(cum * ach_v[g, n * J:(n + 1) * J, :])
                        c_n = cs_v[pl.ds(t * N + n, J, stride=0), :]
                        h_n = hch_v[n * J:(n + 1) * J, :]
                        part.append(c_n * (e * h_n))
                    y_t = y_t + ((part[0] + part[1]) + (part[2] + part[3]))
                ych_v[g, pl.ds(r, J), :] = y_t
            return 0

        hch_v = ich_v.at[pl.ds(0, N * J), :]
        for n in range(N):
            hch_v[n * J:(n + 1) * J, :] = carry_v[pl.ds(c * (J * 2 * N) + half * N + n, J, stride=2 * N), :]
        lax.fori_loop(0, T // UNROLL2, steps, 0)
        in_copy(3, g).wait()
        for j in range(J):
            cols = slice(j * LANES, (j + 1) * LANES)
            y_t = ych_v[g, pl.ds(j, T, stride=J), :]
            y_t = y_t + sk_v[:, pl.ds(off + j * LANES, LANES)] * u_v[g, :, cols].astype(f32)
            out_v[g, :, cols] = (y_t * silu(gate_v[g, :, cols].astype(f32))).astype(bf16)
        out_copy(g).start()

    def second_half(c, _):
        for r in range(1, 8):
            last_copy(c, r).wait_recv()
        finish_group(2 * c, c, 0)
        pl.when(c == 0)(lambda: after_first(C - 1))
        pl.when(c <= 1)(lambda: after_y(C - 2 + c))
        pl.when(c <= 2)(lambda: after_z(C - 3 + c))
        finish_group(2 * c + 1, c, 1)
        return 0

    lax.fori_loop(0, C, second_half, 0)

    for g in range(G):
        out_copy(g).wait()
        halo_copy(g).wait_send()
    for c in range(C):
        for r in range(1, 8):
            first_copy(c, r).wait_send()
            last_copy(c, r).wait_send()
        for r in range(1, 4):
            y_copy(c, r).wait_send()
            z_copy(c, r).wait_send()


ANY = pl.BlockSpec(memory_space=pl.ANY)
UNROLL, UNROLL2 = 8, 8


def local(x_in, gate_in, conv_weight, conv_bias, x_proj, dt_proj, dt_bias, decay_rates, skip_gain):
    vmem, dma = pltpu.VMEM, pltpu.SemaphoreType.DMA
    return pl.pallas_call(
        kernel,
        name="selective_scan",
        out_shape=jax.ShapeDtypeStruct((T, E), bf16),
        in_specs=[ANY] * 9,
        out_specs=ANY,
        scratch_shapes=[
            vmem((G, T, GW), bf16), vmem((G, T, GW), bf16), vmem((KW, E), f32), vmem((1, E), f32),
            vmem((G, R + 2 * N, GW), bf16), vmem((G, R, GW), bf16), vmem((1, E), f32), vmem((N, E), f32), vmem((1, E), f32),
            vmem((G, HALO, GW), bf16), vmem(((HALO + T) * J, LANES), f32), vmem((G, (KW + 1) * J, LANES), f32),
            vmem((G, T, GW), bf16), vmem((T * N, LANES), f32), vmem((T * N, LANES), f32), vmem((G, N * J, LANES), f32),
            vmem((T, R + 2 * N), f32), vmem((ROWS, LANES), f32), vmem((ROWS, LANES), f32),
            vmem((G, ROWS, LANES), f32), vmem((G, ROWS, LANES), f32), vmem((G, T, GW), bf16),
            vmem((C * 8 * AGG, LANES), f32), vmem((C * 8 * AGG, LANES), f32), vmem((C * AGG, LANES), f32),
            vmem((C * 4 * AGG, LANES), f32), vmem((C * AGG, LANES), f32), vmem((C * AGG, LANES), f32),
            vmem((C * 4 * AGG, LANES), f32), vmem((C * 8 * 2 * N, LANES), f32), vmem((C * 8 * 2 * N, LANES), f32),
            dma((4, G)), dma((5,)), dma((G,)), dma((G,)), dma((G,)),
            dma((C, 8)), dma((C, 8)), dma((C, 4)), dma((C, 4)), dma((C, 4)), dma((C, 4)), dma((C, 8)), dma((C, 8))],
        compiler_params=pltpu.CompilerParams(collective_id=0, has_side_effects=True, vmem_limit_bytes=52 * 2**20),
    )(x_in, gate_in, conv_weight, conv_bias.reshape(1, E), x_proj.T, dt_proj, dt_bias.reshape(1, E), decay_rates,
      skip_gain.reshape(1, E))


def solution(mesh):
    tokens = P(("outer", "inner"), None)
    return jax.shard_map(
        local, mesh=mesh, in_specs=(tokens, tokens, P(), P(), P(), P(), P(), P(), P()),
        out_specs=tokens, check_vma=False)
```

time: 282 us -> 84.1 us (0.30)
  other arithmetic: 110 us -> 0 us
  Pallas kernels: 0 us -> 76.3 us
  waiting for transfers between devices: 71.2 us -> 0 us
  blocking collectives: 33.4 us -> 0 us
  local copies, waits for them, and re-layouts: 37.2 us -> 7.31 us
  between operations: 13.5 us -> 0.01 us
  matrix products: 10.1 us -> 0 us
  starting transfers between devices: 4.08 us -> 0 us
    pallas_call x0 -> x1, Pallas kernels: none -> 76.3 us  [local(): pl.pallas_call(kernel, name='selective_scan', out_shape=jax.ShapeDtypeStr...]
    all_gather x4 -> x0, waiting for transfers between devices: 68.7 us -> none  [prefix_by_axis(): pieces = jax.tree.map(lambda part: lax.all_gather(part, axis), running)]
    another operation x16 -> x0, other arithmetic: 40.3 us -> none  [the longest x8 36.6 us: block_step(): running = jnp.cumsum(weighted, axis=0)]
    all_gather x4 -> x0, blocking collectives: 33.4 us -> none  [prefix_by_axis(): pieces = jax.tree.map(lambda part: lax.all_gather(part, axis), running)]
    reduce_sum x8 -> x0, other arithmetic: 21.2 us -> none  [correction(): return jnp.sum(c_blk[:, :, None] * faded, axis=1)]
    add x15 -> x0, other arithmetic: 17.4 us -> none  [the longest x4 11.4 us: combine(): jnp.exp(-later[0][None, :] * decay_rates) * earlier[1] + later[1]]
    neg x11 -> x0, other arithmetic: 11.7 us -> none  [the longest x8 8.61 us: correction(): -cum_blk[:, None, :] * decay_rates[None, :, :]]
    convert_element_type x3 -> x0, other arithmetic: 10.2 us -> none  [the longest x1 5.16 us: local(): (y_full * jax.nn.silu(gate_in.astype(jnp.float32))).astype(jnp.bfloat16)]
  transfers between devices with their start and end apart: 5 -> 0, of which waited for: 5 -> 0; matrix products, arithmetic and copies ran while one was open for 2% -> 0% of each run, Pallas kernels for 0% -> 0%
where the time goes in v2:
time: 84.1 us; the launch traced here: 83.7 us
  Pallas kernels  76.3 us (91%)
  local copies, waits for them, and re-layouts  7.31 us (9%)
    pallas_call x1, Pallas kernels, local(): pl.pallas_call(kernel, name='selective_scan', out_shape=jax.ShapeDtypeStr...  76.3 us
    unnamed x11, local copies, waits for them, and re-layouts  7.31 us

profile of v2, /device:TPU:1, one launch (start us, length us, event | category | flops | bytes accessed | tf_op | source)
XLA Modules:
  0.0 83.7 jit_solution(375799729810425621)
XLA Ops:
  0.0 0.0 copy-start
  0.0 1.0 %copy-done = f32[16,8192]{1,0:T(8,128)S(1)} copy-done((f32[16,8192]{1,0:T(8,128)S(1)}, f32[16,8192]{1,0:T(8,128)}, u32[]{:S(2)}) %copy-start) | copy-done | bytes 524312
  1.0 0.0 copy-start.1
  1.0 0.9 %copy-done.1 = f32[4,8192]{1,0:T(4,128)S(1)} copy-done((f32[4,8192]{1,0:T(4,128)S(1)}, f32[4,8192]{1,0:T(4,128)}, u32[]{:S(2)}) %copy-start.1) | copy-done | bytes 131096
  1.9 0.0 copy-start.2
  1.9 0.8 copy-done.2
  2.7 0.0 copy-start.3
  2.7 0.8 copy-done.3
  3.5 0.0 copy-start.4
  3.5 0.8 copy-done.4
  4.2 76.3 %selective_scan.1 = bf16[128,8192]{1,0:T(8,128)(2,1)} custom-call(bf16[128,8192]{1,0:T(8,128)(2,1)} %x_hbm.1, bf16[128,8192]{1,0:T(8,128)(2,1)} %gate_hbm.1, f32[4,8192]{1,0:T(4,128)S(1)} %copy-done.1, f32[1,8192]{1,0:T(1,128)S(1)} %bitcast.4, bf16[288,8192]{1,0:T(8,128)(2,1)} %bitcast.7, bf16[256,8192]{1,0:T(8,128)(2,1)} %dp_hbm.1, f32[1,8192]{1,0:T(1,128)S(1)} %bitcast.5, ...), custom_call_target="tpu_custom_call" | custom-call | tf_op jit(solution)/shard_map/selective_scan/pallas_call | solution.py:408
  80.6 3.1 %copy.11 = bf16[128,8192]{1,0:T(8,128)(2,1)} copy(bf16[128,8192]{1,0:T(8,128)(2,1)} %selective_scan.1) | data formatting | bytes 4194304
Async XLA Ops:
  0.0 1.0 %copy-start = (f32[16,8192]{1,0:T(8,128)S(1)}, f32[16,8192]{1,0:T(8,128)}, u32[]{:S(2)}) copy-start(f32[16,8192]{1,0:T(8,128)} %a_hbm.1) | copy-start | bytes 1572868
  1.0 0.9 %copy-start.1 = (f32[4,8192]{1,0:T(4,128)S(1)}, f32[4,8192]{1,0:T(4,128)}, u32[]{:S(2)}) copy-start(f32[4,8192]{1,0:T(4,128)} %cw_hbm.1) | copy-start | bytes 393220
  1.9 0.8 copy-start.2
  2.7 0.8 copy-start.3
  3.5 0.8 copy-start.4

commit v3 on v2

--- a/solution.py
+++ b/solution.py
@@ -49,8 +49,8 @@
     return hi, mid, lo
 
 
-def kernel(x_hbm, gate_hbm, cw_hbm, cb_hbm, xp_hbm, dp_hbm, db_hbm, a_hbm, sk_hbm, out_hbm,
-           x_v, gate_v, cw_v, cb_v, xp_v, dp_v, db_v, a_v, sk_v, halo_v, xch_v, wch_v, u_v, bs_v, cs_v, ach_v,
+def kernel(x_hbm, cw_hbm, cb_hbm, xp_hbm, dp_hbm, db_hbm, a_hbm, sk_hbm, out_hbm,
+           x_v, cw_v, cb_v, xp_v, dp_v, db_v, a_v, sk_v, halo_v, xch_v, wch_v, u_v, bs_v, cs_v, ach_v,
            proj_v, dch_v, ich_v, ych_v, cch_v, out_v,
            agg_v, got_v, total_v, ys_v, part_v, ytotal_v, zs_v, back_v, carry_v,
            in_sem, one_sem, out_sem, hsend, hrecv, send1, recv1, sendy, recvy, sendz, recvz, send4, recv4):
@@ -61,22 +61,18 @@
 
     def in_copy(kind, g):
         cols = pl.ds(pl.multiple_of(g * GW, GW), GW)
-        source, target = ((x_hbm, x_v), (xp_hbm, xp_v), (dp_hbm, dp_v), (gate_hbm, gate_v))[kind]
+        source, target = ((x_hbm, x_v), (xp_hbm, xp_v), (dp_hbm, dp_v))[kind]
         return pltpu.make_async_copy(source.at[:, cols], target.at[g], in_sem.at[kind, g])
 
     ones = [pltpu.make_async_copy(s, t, one_sem.at[k]) for k, (s, t) in enumerate(
         ((cw_hbm, cw_v), (cb_hbm, cb_v), (a_hbm, a_v), (db_hbm, db_v), (sk_hbm, sk_v)))]
     for cp in ones[:2]:
         cp.start()
-    for g in range(G):
+    for g in range(AHEAD):
         in_copy(0, g).start()
         in_copy(1, g).start()
     for cp in ones[2:]:
         cp.start()
-    for g in range(G):
-        in_copy(2, g).start()
-    for g in range(G):
-        in_copy(3, g).start()
 
     def at_line(v):
         return (v // 4, v % 4)
@@ -148,6 +144,12 @@
         wch_v[g, KW * J + j:KW * J + j + 1, :] = cb_v[:, cols]
 
     def conv_group(g, _):
+        @pl.when(g + AHEAD < G)
+        def _():
+            in_copy(0, g + AHEAD).start()
+            in_copy(1, g + AHEAD).start()
+
+        in_copy(2, g).start()
         in_copy(0, g).wait()
         halo_copy(g).wait_recv()
         for j in range(J):
@@ -163,12 +165,12 @@
                 acc = w[KW]
                 for i in range(KW):
                     acc = acc + w[i] * xch_v[pl.ds(r + (HALO - KW + 1 + i) * J, J), :]
-                dch_v[pl.ds(r, J), :] = silu(acc)
+                dch_v[0, pl.ds(r, J), :] = silu(acc)
             return 0
 
         lax.fori_loop(0, T // 16, tokens, 0)
         for j in range(J):
-            u_v[g, :, j * LANES:(j + 1) * LANES] = dch_v[pl.ds(j, T, stride=J), :].astype(bf16)
+            u_v[g, :, j * LANES:(j + 1) * LANES] = dch_v[0, pl.ds(j, T, stride=J), :].astype(bf16)
         in_copy(1, g).wait()
         proj_v[...] += lax.dot_general(u_v[g], xp_v[g], (((1,), (1,)), ((), ())), preferred_element_type=f32)
         return 0
@@ -205,7 +207,7 @@
     for q in range(E // LANES):
         ach_v[q // J, pl.ds(q % J, N, stride=J), :] = a_v[:, q * LANES:(q + 1) * LANES] * -LOG2E
 
-    def scan_group(g, c, half):
+    def steps_of(g, slot):
         off = pl.multiple_of(g * GW, GW)
         in_copy(2, g).wait()
         dt_low = proj_v[:, 0:R].astype(bf16)
@@ -215,37 +217,60 @@
             i = d * u_v[g, :, s:s + 256].astype(f32)
             for h in range(2):
                 j = s // LANES + h
-                dch_v[pl.ds(j, T, stride=J), :] = d[:, h * LANES:(h + 1) * LANES]
-                ich_v[pl.ds(j, T, stride=J), :] = i[:, h * LANES:(h + 1) * LANES]
-
+                dch_v[slot, pl.ds(j, T, stride=J), :] = d[:, h * LANES:(h + 1) * LANES]
+                ich_v[slot, pl.ds(j, T, stride=J), :] = i[:, h * LANES:(h + 1) * LANES]
+
+    def recur(g, slot, h, cum, unroll, emit):
         def steps(k, carry):
             h, cum = list(carry[0]), carry[1]
-            for tt in range(UNROLL):
-                t = k * UNROLL + tt
+            for tt in range(unroll):
+                t = k * unroll + tt
                 r = pl.multiple_of(t * J, J)
-                d = dch_v[pl.ds(r, J), :]
-                i = ich_v[pl.ds(r, J), :]
-                cum = cum + d
-                cch_v[g, pl.ds(r, J), :] = cum
+                d = dch_v[slot, pl.ds(r, J), :]
+                i = ich_v[slot, pl.ds(r, J), :]
+                if cum is not None:
+                    cum = cum + d
                 ys = []
                 for n in range(N):
                     e = jnp.exp2(d * ach_v[g, n * J:(n + 1) * J, :])
                     b = bs_v[pl.ds(t * N + n, J, stride=0), :]
-                    c_n = cs_v[pl.ds(t * N + n, J, stride=0), :]
                     h[n] = e * h[n] + b * i
-                    ys.append(c_n * h[n])
-                    if n % 4 == 3:
-                        y4 = (ys[0] + ys[1]) + (ys[2] + ys[3])
-                        y_t = y4 if n == 3 else y_t + y4
-                        ys = []
-                ych_v[g, pl.ds(r, J), :] = y_t
+                    if emit is not None:
+                        ys.append(cs_v[pl.ds(t * N + n, J, stride=0), :] * h[n])
+                        if n % 4 == 3:
+                            y4 = (ys[0] + ys[1]) + (ys[2] + ys[3])
+                            y_t = y4 if n == 3 else y_t + y4
+                            ys = []
+                if emit is not None:
+                    emit(r, y_t, cum)
             return tuple(h), cum
 
-        zero = jnp.zeros((J, LANES), f32)
-        h, cum = lax.fori_loop(0, T // UNROLL, steps, ((zero,) * N, zero))
+        return lax.fori_loop(0, T // unroll, steps, (tuple(h), cum))
+
+    zero = jnp.zeros((J, LANES), f32)
+
+    def aggregate(c, half, h, cum):
         for n in range(N):
             agg_v[pl.ds(c * (J * AGG) + half * N + n, J, stride=AGG), :] = h[n]
         agg_v[pl.ds(c * (J * AGG) + 2 * N + half, J, stride=AGG), :] = cum
+
+    def carried(c, half, n):
+        return carry_v[pl.ds(c * (J * 2 * N) + half * N + n, J, stride=2 * N), :]
+
+    def final_state(p, half):
+        g = 2 * p + half
+        steps_of(g, g)
+        aggregate(p, half, *recur(g, g, (zero,) * N, zero, UNROLL_S, None))
+
+    def from_zero(p, half):
+        g = 2 * p + half
+        steps_of(g, G // 2)
+
+        def emit(r, y_t, cum):
+            ych_v[g, pl.ds(r, J), :] = y_t
+            cch_v[g - G // 2, pl.ds(r, J), :] = cum
+
+        aggregate(p, half, *recur(g, G // 2, (zero,) * N, zero, UNROLL_L, emit))
 
     def rates(c, half):
         col = pl.multiple_of((c * 2 + half) * GW + me * LANES, LANES)
@@ -328,64 +353,82 @@
         for r in range(1, 8):
             last_copy(c, r).start()
 
-    def first_half(p, _):
-        scan_group(2 * p, p, 0)
-        pl.when(p >= 1)(lambda: after_first(p - 1))
-        pl.when(p >= 2)(lambda: after_y(p - 2))
-        pl.when(p >= 3)(lambda: after_z(p - 3))
-        scan_group(2 * p + 1, p, 1)
-        send_first(p)
-        return 0
-
-    lax.fori_loop(0, C, first_half, 0)
-
     def out_copy(g):
         cols = pl.ds(pl.multiple_of(g * GW, GW), GW)
         return pltpu.make_async_copy(out_v.at[g], out_hbm.at[:, cols], out_sem.at[g])
 
-    def finish_group(g, c, half):
+    def finish(g):
         off = pl.multiple_of(g * GW, GW)
+        for j in range(J):
+            cols = slice(j * LANES, (j + 1) * LANES)
+            y_t = ych_v[g, pl.ds(j, T, stride=J), :]
+            out_v[g, :, cols] = y_t + sk_v[:, pl.ds(off + j * LANES, LANES)] * u_v[g, :, cols].astype(f32)
+        out_copy(g).start()
+
+    def wait_carry(c):
+        for r in range(1, 8):
+            last_copy(c, r).wait_recv()
+
+    def from_carry(p, half):
+        c = p - C
+        g = 2 * c + half
+        if half == 0:
+            wait_carry(c)
+
+        def emit(r, y_t, cum):
+            ych_v[g, pl.ds(r, J), :] = y_t
+
+        recur(g, g, [carried(c, half, n) for n in range(N)], None, UNROLL_F, emit)
+        finish(g)
+
+    def add_carry(p, half):
+        c = p - C
+        g = 2 * c + half
+        if half == 0:
+            wait_carry(c)
+        hch_v = dch_v.at[0, pl.ds(0, N * J), :]
+        for n in range(N):
+            hch_v[n * J:(n + 1) * J, :] = carried(c, half, n)
 
         def steps(k, _):
-            for tt in range(UNROLL2):
-                t = k * UNROLL2 + tt
+            for tt in range(UNROLL_C):
+                t = k * UNROLL_C + tt
                 r = pl.multiple_of(t * J, J)
-                cum = cch_v[g, pl.ds(r, J), :]
+                cum = cch_v[g - G // 2, pl.ds(r, J), :]
                 y_t = ych_v[g, pl.ds(r, J), :]
                 for n4 in range(0, N, 4):
                     part = []
                     for n in range(n4, n4 + 4):
                         e = jnp.exp2(cum * ach_v[g, n * J:(n + 1) * J, :])
                         c_n = cs_v[pl.ds(t * N + n, J, stride=0), :]
-                        h_n = hch_v[n * J:(n + 1) * J, :]
-                        part.append(c_n * (e * h_n))
+                        part.append(c_n * (e * hch_v[n * J:(n + 1) * J, :]))
                     y_t = y_t + ((part[0] + part[1]) + (part[2] + part[3]))
                 ych_v[g, pl.ds(r, J), :] = y_t
             return 0
 
-        hch_v = ich_v.at[pl.ds(0, N * J), :]
-        for n in range(N):
-            hch_v[n * J:(n + 1) * J, :] = carry_v[pl.ds(c * (J * 2 * N) + half * N + n, J, stride=2 * N), :]
-        lax.fori_loop(0, T // UNROLL2, steps, 0)
-        in_copy(3, g).wait()
-        for j in range(J):
-            cols = slice(j * LANES, (j + 1) * LANES)
-            y_t = ych_v[g, pl.ds(j, T, stride=J), :]
-            y_t = y_t + sk_v[:, pl.ds(off + j * LANES, LANES)] * u_v[g, :, cols].astype(f32)
-            out_v[g, :, cols] = (y_t * silu(gate_v[g, :, cols].astype(f32))).astype(bf16)
-        out_copy(g).start()
-
-    def second_half(c, _):
-        for r in range(1, 8):
-            last_copy(c, r).wait_recv()
-        finish_group(2 * c, c, 0)
-        pl.when(c == 0)(lambda: after_first(C - 1))
-        pl.when(c <= 1)(lambda: after_y(C - 2 + c))
-        pl.when(c <= 2)(lambda: after_z(C - 3 + c))
-        finish_group(2 * c + 1, c, 1)
-        return 0
-
-    lax.fori_loop(0, C, second_half, 0)
+        lax.fori_loop(0, T // UNROLL_C, steps, 0)
+        finish(g)
+
+    def pair(work, lo, hi):
+        def body(p, _):
+            work(p, 0)
+            if hi > 2 and lo < C + 2:
+                pl.when((p >= 2) & (p < C + 2))(lambda: after_y(p - 2))
+            work(p, 1)
+            if hi <= C:
+                send_first(p)
+            if hi > 1 and lo <= C:
+                pl.when((p >= 1) & (p <= C))(lambda: after_first(p - 1))
+            if hi > 2 and lo < C + 2:
+                pl.when((p >= 2) & (p < C + 2))(lambda: after_z(p - 2))
+            return 0
+
+        lax.fori_loop(lo, hi, body, 0)
+
+    pair(final_state, 0, C // 2)
+    pair(from_zero, C // 2, C)
+    pair(from_carry, C, C + C // 2)
+    pair(add_carry, C + C // 2, 2 * C)
 
     for g in range(G):
         out_copy(g).wait()
@@ -399,33 +442,35 @@
             z_copy(c, r).wait_send()
 
 
-ANY = pl.BlockSpec(memory_space=pl.ANY)
-UNROLL, UNROLL2 = 8, 8
+HBM = pl.BlockSpec(memory_space=pltpu.HBM)
+UNROLL_S, UNROLL_L, UNROLL_F, UNROLL_C = 16, 16, 16, 16
+AHEAD = 3
 
 
 def local(x_in, gate_in, conv_weight, conv_bias, x_proj, dt_proj, dt_bias, decay_rates, skip_gain):
     vmem, dma = pltpu.VMEM, pltpu.SemaphoreType.DMA
-    return pl.pallas_call(
+    y = pl.pallas_call(
         kernel,
         name="selective_scan",
-        out_shape=jax.ShapeDtypeStruct((T, E), bf16),
-        in_specs=[ANY] * 9,
-        out_specs=ANY,
+        out_shape=jax.ShapeDtypeStruct((T, E), f32),
+        in_specs=[HBM] * 8,
+        out_specs=HBM,
         scratch_shapes=[
-            vmem((G, T, GW), bf16), vmem((G, T, GW), bf16), vmem((KW, E), f32), vmem((1, E), f32),
+            vmem((G, T, GW), bf16), vmem((KW, E), f32), vmem((1, E), f32),
             vmem((G, R + 2 * N, GW), bf16), vmem((G, R, GW), bf16), vmem((1, E), f32), vmem((N, E), f32), vmem((1, E), f32),
             vmem((G, HALO, GW), bf16), vmem(((HALO + T) * J, LANES), f32), vmem((G, (KW + 1) * J, LANES), f32),
             vmem((G, T, GW), bf16), vmem((T * N, LANES), f32), vmem((T * N, LANES), f32), vmem((G, N * J, LANES), f32),
-            vmem((T, R + 2 * N), f32), vmem((ROWS, LANES), f32), vmem((ROWS, LANES), f32),
-            vmem((G, ROWS, LANES), f32), vmem((G, ROWS, LANES), f32), vmem((G, T, GW), bf16),
+            vmem((T, R + 2 * N), f32), vmem((G // 2 + 1, ROWS, LANES), f32), vmem((G // 2 + 1, ROWS, LANES), f32),
+            vmem((G, ROWS, LANES), f32), vmem((G // 2, ROWS, LANES), f32), vmem((G, T, GW), f32),
             vmem((C * 8 * AGG, LANES), f32), vmem((C * 8 * AGG, LANES), f32), vmem((C * AGG, LANES), f32),
             vmem((C * 4 * AGG, LANES), f32), vmem((C * AGG, LANES), f32), vmem((C * AGG, LANES), f32),
             vmem((C * 4 * AGG, LANES), f32), vmem((C * 8 * 2 * N, LANES), f32), vmem((C * 8 * 2 * N, LANES), f32),
-            dma((4, G)), dma((5,)), dma((G,)), dma((G,)), dma((G,)),
+            dma((3, G)), dma((5,)), dma((G,)), dma((G,)), dma((G,)),
             dma((C, 8)), dma((C, 8)), dma((C, 4)), dma((C, 4)), dma((C, 4)), dma((C, 4)), dma((C, 8)), dma((C, 8))],
-        compiler_params=pltpu.CompilerParams(collective_id=0, has_side_effects=True, vmem_limit_bytes=52 * 2**20),
-    )(x_in, gate_in, conv_weight, conv_bias.reshape(1, E), x_proj.T, dt_proj, dt_bias.reshape(1, E), decay_rates,
+        compiler_params=pltpu.CompilerParams(collective_id=0, has_side_effects=True, vmem_limit_bytes=60 * 2**20),
+    )(x_in, conv_weight, conv_bias.reshape(1, E), x_proj.T, dt_proj, dt_bias.reshape(1, E), decay_rates,
       skip_gain.reshape(1, E))
+    return (y * jax.nn.silu(gate_in.astype(f32))).astype(bf16)
 
 
 def solution(mesh):

time: 84.1 us -> 72.8 us (0.87)
  Pallas kernels: 76.3 us -> 67.9 us
  local copies, waits for them, and re-layouts: 7.31 us -> 0.01 us
  other arithmetic: 0 us -> 4.68 us
    pallas_call x1, Pallas kernels: 76.3 us -> 67.9 us  [local(): pl.pallas_call(kernel, name='selective_scan', out_shape=jax.ShapeDtypeStr...]
    unnamed x11 -> x2, local copies, waits for them, and re-layouts: 7.31 us -> 0.01 us
    convert_element_type x0 -> x1, other arithmetic: none -> 4.68 us  [local(): return (y * jax.nn.silu(gate_in.astype(f32))).astype(bf16)]
where the time goes in v3:
time: 72.8 us; the launch traced here: 72.6 us
  Pallas kernels  67.9 us (93%)
  other arithmetic  4.68 us (6%)
    pallas_call x1, Pallas kernels, local(): pl.pallas_call(kernel, name='selective_scan', out_shape=jax.ShapeDtypeStr...  67.9 us
    convert_element_type x1, other arithmetic, local(): return (y * jax.nn.silu(gate_in.astype(f32))).astype(bf16)  4.68 us

profile of v3, /device:TPU:1, one launch (start us, length us, event | category | flops | bytes accessed | tf_op | source)
XLA Modules:
  0.0 72.6 jit_solution(8423022788292686676)
XLA Ops:
  0.0 0.0 copy-start
  0.0 67.9 %selective_scan.1 = f32[128,8192]{1,0:T(8,128)} custom-call(bf16[128,8192]{1,0:T(8,128)(2,1)} %x_hbm.1, f32[4,8192]{1,0:T(4,128)} %cw_hbm.1, f32[1,8192]{1,0:T(1,128)} %bitcast.5, bf16[288,8192]{1,0:T(8,128)(2,1)} %bitcast.4, bf16[256,8192]{1,0:T(8,128)(2,1)} %dp_hbm.1, f32[1,8192]{1,0:T(1,128)} %bitcast.6, f32[16,8192]{1,0:T(8,128)} %a_hbm.1, f32[1,8192]{1,0:T(1,128)} %bitcast.7), custom_call_target="tpu_custom_call" | custom-call | tf_op jit(solution)/shard_map/selective_scan/pallas_call | solution.py:452
  67.9 0.0 copy-done
  67.9 4.7 %fusion.4 = bf16[128,8192]{1,0:T(8,128)(2,1)} fusion(f32[128,8192]{1,0:T(8,128)} %selective_scan.1, bf16[128,8192]{1,0:T(8,128)(2,1)S(1)} %copy-done), kind=kLoop, calls=%fused_computation.6 | loop fusion | flops 7340032 | bytes 8388608 | tf_op jit(solution)/shard_map/convert_element_type | solution.py:473
Async XLA Ops:
  0.0 67.9 %copy-start = (bf16[128,8192]{1,0:T(8,128)(2,1)S(1)}, bf16[128,8192]{1,0:T(8,128)(2,1)}, u32[]{:S(2)}) copy-start(bf16[128,8192]{1,0:T(8,128)(2,1)} %param.10) | copy-start | bytes 6291460

commit v4 on v3

--- a/solution.py
+++ b/solution.py
@@ -68,11 +68,12 @@
         ((cw_hbm, cw_v), (cb_hbm, cb_v), (a_hbm, a_v), (db_hbm, db_v), (sk_hbm, sk_v)))]
     for cp in ones[:2]:
         cp.start()
-    for g in range(AHEAD):
+    for g in range(G):
         in_copy(0, g).start()
-        in_copy(1, g).start()
     for cp in ones[2:]:
         cp.start()
+    for g in range(AHEAD):
+        in_copy(1, g).start()
 
     def at_line(v):
         return (v // 4, v % 4)
@@ -96,16 +97,12 @@
     for r in range(1, 4):
         pl.semaphore_signal(barrier, inc=1, device_id=at_y((y + r) % 4), device_id_type=MESH)
         pl.semaphore_signal(barrier, inc=1, device_id=at_z((z + r) % 4), device_id_type=MESH)
-    pl.semaphore_wait(barrier, 15)
 
     def halo_copy(g):
         cols = pl.ds(pl.multiple_of(g * GW, GW), GW)
         return pltpu.make_async_remote_copy(
             src_ref=x_hbm.at[pl.ds(T - HALO, HALO), cols], dst_ref=halo_v.at[g], send_sem=hsend.at[g],
             recv_sem=hrecv.at[g], device_id=at_line(after), device_id_type=MESH)
-
-    for g in range(G):
-        halo_copy(g).start()
 
     def rows(index, count):
         return pl.ds(pl.multiple_of(index * count, 8), count)
@@ -143,39 +140,61 @@
         wch_v[g, pl.ds(j, KW, stride=J), :] = cw_v[:, cols]
         wch_v[g, KW * J + j:KW * J + j + 1, :] = cb_v[:, cols]
 
-    def conv_group(g, _):
+    def conv_tokens(g, k):
+        w = [wch_v[g, i * J:(i + 1) * J, :] for i in range(KW + 1)]
+        for tt in range(16):
+            r = pl.multiple_of((k * 16 + tt) * J, J)
+            acc = w[KW]
+            for i in range(KW):
+                acc = acc + w[i] * xch_v[g, pl.ds(r + (HALO - KW + 1 + i) * J, J), :]
+            dch_v[0, pl.ds(r, J), :] = silu(acc)
+
+    def conv_later(g):
         @pl.when(g + AHEAD < G)
         def _():
-            in_copy(0, g + AHEAD).start()
             in_copy(1, g + AHEAD).start()
 
+        in_copy(0, g).wait()
+        for j in range(J):
+            xch_v[g, pl.ds(HALO * J + j, T, stride=J), :] = x_v[g, :, j * LANES:(j + 1) * LANES].astype(f32)
+
+        def tokens(k, _):
+            conv_tokens(g, k)
+            return 0
+
+        lax.fori_loop(1, T // 16, tokens, 0)
+        for j in range(J):
+            late = dch_v[0, pl.ds(16 * J + j, T - 16, stride=J), :]
+            u_v[g, 16:T, j * LANES:(j + 1) * LANES] = late.astype(bf16)
+
+    def conv_first(g, _):
         in_copy(2, g).start()
-        in_copy(0, g).wait()
         halo_copy(g).wait_recv()
         for j in range(J):
-            cols = slice(j * LANES, (j + 1) * LANES)
-            halo = halo_v[g, :, cols].astype(f32)
-            xch_v[pl.ds(j, HALO, stride=J), :] = jnp.where(line > 0, halo, 0.0)
-            xch_v[pl.ds(HALO * J + j, T, stride=J), :] = x_v[g, :, cols].astype(f32)
-
-        def tokens(k, _):
-            w = [wch_v[g, i * J:(i + 1) * J, :] for i in range(KW + 1)]
-            for tt in range(16):
-                r = pl.multiple_of((k * 16 + tt) * J, J)
-                acc = w[KW]
-                for i in range(KW):
-                    acc = acc + w[i] * xch_v[pl.ds(r + (HALO - KW + 1 + i) * J, J), :]
-                dch_v[0, pl.ds(r, J), :] = silu(acc)
-            return 0
-
-        lax.fori_loop(0, T // 16, tokens, 0)
+            halo = halo_v[g, :, j * LANES:(j + 1) * LANES].astype(f32)
+            xch_v[g, pl.ds(j, HALO, stride=J), :] = jnp.where(line > 0, halo, 0.0)
+        conv_tokens(g, 0)
         for j in range(J):
-            u_v[g, :, j * LANES:(j + 1) * LANES] = dch_v[0, pl.ds(j, T, stride=J), :].astype(bf16)
+            u_v[g, 0:16, j * LANES:(j + 1) * LANES] = dch_v[0, pl.ds(j, 16, stride=J), :].astype(bf16)
         in_copy(1, g).wait()
         proj_v[...] += lax.dot_general(u_v[g], xp_v[g], (((1,), (1,)), ((), ())), preferred_element_type=f32)
         return 0
 
-    lax.fori_loop(0, G, conv_group, 0)
+    conv_later(0)
+    pl.semaphore_wait(barrier, 15)
+    for g in range(G):
+        halo_copy(g).start()
+
+    def rest(g, _):
+        conv_later(g)
+        return 0
+
+    lax.fori_loop(1, G, rest, 0)
+    for cp in ones[2:]:
+        cp.wait()
+    for q in range(E // LANES):
+        ach_v[q // J, pl.ds(q % J, N, stride=J), :] = a_v[:, q * LANES:(q + 1) * LANES] * -LOG2E
+    lax.fori_loop(0, G, conv_first, 0)
 
     row = lax.broadcasted_iota(jnp.int32, (256, 16), 0)
     col = lax.broadcasted_iota(jnp.int32, (256, 16), 1)
@@ -201,11 +220,6 @@
         return 0
 
     lax.fori_loop(0, T // 16, spread, 0)
-
-    for cp in ones[2:]:
-        cp.wait()
-    for q in range(E // LANES):
-        ach_v[q // J, pl.ds(q % J, N, stride=J), :] = a_v[:, q * LANES:(q + 1) * LANES] * -LOG2E
 
     def steps_of(g, slot):
         off = pl.multiple_of(g * GW, GW)
@@ -458,7 +472,7 @@
         scratch_shapes=[
             vmem((G, T, GW), bf16), vmem((KW, E), f32), vmem((1, E), f32),
             vmem((G, R + 2 * N, GW), bf16), vmem((G, R, GW), bf16), vmem((1, E), f32), vmem((N, E), f32), vmem((1, E), f32),
-            vmem((G, HALO, GW), bf16), vmem(((HALO + T) * J, LANES), f32), vmem((G, (KW + 1) * J, LANES), f32),
+            vmem((G, HALO, GW), bf16), vmem((G, (HALO + T) * J, LANES), f32), vmem((G, (KW + 1) * J, LANES), f32),
             vmem((G, T, GW), bf16), vmem((T * N, LANES), f32), vmem((T * N, LANES), f32), vmem((G, N * J, LANES), f32),
             vmem((T, R + 2 * N), f32), vmem((G // 2 + 1, ROWS, LANES), f32), vmem((G // 2 + 1, ROWS, LANES), f32),
             vmem((G, ROWS, LANES), f32), vmem((G // 2, ROWS, LANES), f32), vmem((G, T, GW), f32),
@@ -470,7 +484,8 @@
         compiler_params=pltpu.CompilerParams(collective_id=0, has_side_effects=True, vmem_limit_bytes=60 * 2**20),
     )(x_in, conv_weight, conv_bias.reshape(1, E), x_proj.T, dt_proj, dt_bias.reshape(1, E), decay_rates,
       skip_gain.reshape(1, E))
-    return (y * jax.nn.silu(gate_in.astype(f32))).astype(bf16)
+    gate = gate_in.astype(f32)
+    return (y * (gate * (0.5 * jnp.tanh(0.5 * gate) + 0.5))).astype(bf16)
 
 
 def solution(mesh):

time: 72.8 us -> 69.1 us (0.949)
  Pallas kernels: 67.9 us -> 64.4 us
    pallas_call x1, Pallas kernels: 67.9 us -> 64.4 us  [local(): pl.pallas_call(kernel, name='selective_scan', out_shape=jax.ShapeDtypeStr...]
where the time goes in v4:
time: 69.1 us; the launch traced here: 69 us
  Pallas kernels  64.4 us (93%)
  other arithmetic  4.53 us (7%)
    pallas_call x1, Pallas kernels, local(): pl.pallas_call(kernel, name='selective_scan', out_shape=jax.ShapeDtypeStr...  64.4 us
    convert_element_type x1, other arithmetic, local(): return (y * (gate * (0.5 * jnp.tanh(0.5 * gate) + 0.5))).astype(bf16)  4.53 us

profile of v4, /device:TPU:1, one launch (start us, length us, event | category | flops | bytes accessed | tf_op | source)
XLA Modules:
  0.0 69.0 jit_solution(7343643660997455337)
XLA Ops:
  0.0 0.0 copy-start
  0.0 64.4 %selective_scan.1 = f32[128,8192]{1,0:T(8,128)} custom-call(bf16[128,8192]{1,0:T(8,128)(2,1)} %x_hbm.1, f32[4,8192]{1,0:T(4,128)} %cw_hbm.1, f32[1,8192]{1,0:T(1,128)} %bitcast.5, bf16[288,8192]{1,0:T(8,128)(2,1)} %bitcast.4, bf16[256,8192]{1,0:T(8,128)(2,1)} %dp_hbm.1, f32[1,8192]{1,0:T(1,128)} %bitcast.6, f32[16,8192]{1,0:T(8,128)} %a_hbm.1, f32[1,8192]{1,0:T(1,128)} %bitcast.7), custom_call_target="tpu_custom_call" | custom-call | tf_op jit(solution)/shard_map/selective_scan/pallas_call | solution.py:466
  64.4 0.0 copy-done
  64.5 4.5 %fusion.4 = bf16[128,8192]{1,0:T(8,128)(2,1)} fusion(f32[128,8192]{1,0:T(8,128)} %selective_scan.1, bf16[128,8192]{1,0:T(8,128)(2,1)S(1)} %copy-done), kind=kLoop, calls=%fused_computation.6 | loop fusion | flops 7340032 | bytes 8388608 | tf_op jit(solution)/shard_map/convert_element_type | solution.py:488
Async XLA Ops:
  0.0 64.4 %copy-start = (bf16[128,8192]{1,0:T(8,128)(2,1)S(1)}, bf16[128,8192]{1,0:T(8,128)(2,1)}, u32[]{:S(2)}) copy-start(bf16[128,8192]{1,0:T(8,128)(2,1)} %param.10) | copy-start | bytes 6291460

commit v5 on v4

--- a/solution.py
+++ b/solution.py
@@ -219,7 +219,7 @@
         cs_v[pl.ds(r, 256), :] = full[:, LANES:]
         return 0
 
-    lax.fori_loop(0, T // 16, spread, 0)
+    lax.fori_loop(0, T // 16, spread, 0, unroll=True)
 
     def steps_of(g, slot):
         off = pl.multiple_of(g * GW, GW)
@@ -444,9 +444,6 @@
     pair(from_carry, C, C + C // 2)
     pair(add_carry, C + C // 2, 2 * C)
 
-    for g in range(G):
-        out_copy(g).wait()
-        halo_copy(g).wait_send()
     for c in range(C):
         for r in range(1, 8):
             first_copy(c, r).wait_send()
@@ -454,9 +451,12 @@
         for r in range(1, 4):
             y_copy(c, r).wait_send()
             z_copy(c, r).wait_send()
-
-
-HBM = pl.BlockSpec(memory_space=pltpu.HBM)
+    for g in range(G):
+        halo_copy(g).wait_send()
+        out_copy(g).wait()
+
+
+ANY = pl.BlockSpec(memory_space=pl.ANY)
 UNROLL_S, UNROLL_L, UNROLL_F, UNROLL_C = 16, 16, 16, 16
 AHEAD = 3
 
@@ -466,9 +466,9 @@
     y = pl.pallas_call(
         kernel,
         name="selective_scan",
-        out_shape=jax.ShapeDtypeStruct((T, E), f32),
-        in_specs=[HBM] * 8,
-        out_specs=HBM,
+        out_shape=pltpu.VMEM((T, E), f32),
+        in_specs=[ANY] * 8,
+        out_specs=ANY,
         scratch_shapes=[
             vmem((G, T, GW), bf16), vmem((KW, E), f32), vmem((1, E), f32),
             vmem((G, R + 2 * N, GW), bf16), vmem((G, R, GW), bf16), vmem((1, E), f32), vmem((N, E), f32), vmem((1, E), f32),
@@ -481,9 +481,10 @@
             vmem((C * 4 * AGG, LANES), f32), vmem((C * 8 * 2 * N, LANES), f32), vmem((C * 8 * 2 * N, LANES), f32),
             dma((3, G)), dma((5,)), dma((G,)), dma((G,)), dma((G,)),
             dma((C, 8)), dma((C, 8)), dma((C, 4)), dma((C, 4)), dma((C, 4)), dma((C, 4)), dma((C, 8)), dma((C, 8))],
-        compiler_params=pltpu.CompilerParams(collective_id=0, has_side_effects=True, vmem_limit_bytes=60 * 2**20),
-    )(x_in, conv_weight, conv_bias.reshape(1, E), x_proj.T, dt_proj, dt_bias.reshape(1, E), decay_rates,
-      skip_gain.reshape(1, E))
+        compiler_params=pltpu.CompilerParams(collective_id=0, has_side_effects=True, vmem_limit_bytes=52 * 2**20),
+    )(*(pltpu.with_memory_space_constraint(v, pltpu.HBM) for v in (
+        x_in, conv_weight, conv_bias.reshape(1, E), x_proj.T, dt_proj, dt_bias.reshape(1, E), decay_rates,
+        skip_gain.reshape(1, E))))
     gate = gate_in.astype(f32)
     return (y * (gate * (0.5 * jnp.tanh(0.5 * gate) + 0.5))).astype(bf16)
 

time: 69.1 us -> 64.2 us (0.929)
  Pallas kernels: 64.4 us -> 61.7 us
  other arithmetic: 4.53 us -> 2.34 us
    pallas_call x1, Pallas kernels: 64.4 us -> 61.7 us  [local(): pl.pallas_call(kernel, name='selective_scan', out_shape=pltpu.VMEM((T, E)...]
    convert_element_type x1, other arithmetic: 4.53 us -> 2.34 us  [local(): return (y * (gate * (0.5 * jnp.tanh(0.5 * gate) + 0.5))).astype(bf16)]
where the time goes in v5:
time: 64.2 us; the launch traced here: 64.1 us
  Pallas kernels  61.7 us (96%)
  other arithmetic  2.34 us (4%)
    pallas_call x1, Pallas kernels, local(): pl.pallas_call(kernel, name='selective_scan', out_shape=pltpu.VMEM((T, E)...  61.7 us
    convert_element_type x1, other arithmetic, local(): return (y * (gate * (0.5 * jnp.tanh(0.5 * gate) + 0.5))).astype(bf16)  2.34 us

profile of v5, /device:TPU:1, one launch (start us, length us, event | category | flops | bytes accessed | tf_op | source)
XLA Modules:
  0.0 64.1 jit_solution(7899734551611082809)
XLA Ops:
  0.0 0.0 copy-start
  0.0 61.7 %selective_scan.1 = f32[128,8192]{1,0:T(8,128)S(1)} custom-call(bf16[128,8192]{1,0:T(8,128)(2,1)} %x_hbm.1, f32[4,8192]{1,0:T(4,128)} %cw_hbm.1, f32[1,8192]{1,0:T(1,128)} %bitcast.5, bf16[288,8192]{1,0:T(8,128)(2,1)} %bitcast.4, bf16[256,8192]{1,0:T(8,128)(2,1)} %dp_hbm.1, f32[1,8192]{1,0:T(1,128)} %bitcast.6, f32[16,8192]{1,0:T(8,128)} %a_hbm.1, ...), custom_call_target="tpu_custom_call" | custom-call | tf_op jit(solution)/shard_map/selective_scan/pallas_call | solution.py:466
  61.7 0.0 copy-done
  61.7 2.3 %fusion.4 = bf16[128,8192]{1,0:T(8,128)(2,1)} fusion(f32[128,8192]{1,0:T(8,128)S(1)} %selective_scan.1, bf16[128,8192]{1,0:T(8,128)(2,1)S(1)} %copy-done), kind=kLoop, calls=%fused_computation.6 | loop fusion | flops 7340032 | bytes 8388608 | tf_op jit(solution)/shard_map/convert_element_type | solution.py:489
Async XLA Ops:
  0.0 61.7 %copy-start = (bf16[128,8192]{1,0:T(8,128)(2,1)S(1)}, bf16[128,8192]{1,0:T(8,128)(2,1)}, u32[]{:S(2)}) copy-start(bf16[128,8192]{1,0:T(8,128)(2,1)} %param.10) | copy-start | bytes 6291460

commit v6 on v5

--- a/solution.py
+++ b/solution.py
@@ -52,10 +52,10 @@
 def kernel(x_hbm, cw_hbm, cb_hbm, xp_hbm, dp_hbm, db_hbm, a_hbm, sk_hbm, out_hbm,
            x_v, cw_v, cb_v, xp_v, dp_v, db_v, a_v, sk_v, halo_v, xch_v, wch_v, u_v, bs_v, cs_v, ach_v,
            proj_v, dch_v, ich_v, ych_v, cch_v, out_v,
-           agg_v, got_v, total_v, ys_v, part_v, ytotal_v, zs_v, back_v, carry_v,
-           in_sem, one_sem, out_sem, hsend, hrecv, send1, recv1, sendy, recvy, sendz, recvz, send4, recv4):
+           agg_v, got_v, total_v, all_v, back_v, carry_v,
+           in_sem, one_sem, out_sem, hsend, hrecv, send1, recv1, send2, recv2, send4, recv4):
     outer, x = lax.axis_index("outer"), lax.axis_index("inner")
-    core, y, z = outer % 2, (outer // 2) % 4, outer // 8
+    core, mine = outer % 2, outer // 2
     me = core * 4 + x
     line = outer * 4 + x
 
@@ -79,13 +79,10 @@
         return (v // 4, v % 4)
 
     def member(m):
-        return ((z * 4 + y) * 2 + m // 4, m % 4)
-
-    def at_y(v):
-        return ((z * 4 + v) * 2 + core, x)
-
-    def at_z(v):
-        return ((v * 4 + y) * 2 + core, x)
+        return (mine * 2 + m // 4, m % 4)
+
+    def peer(v):
+        return (v * 2 + core, x)
 
     devices = lax.axis_size("outer") * lax.axis_size("inner")
     barrier = pltpu.get_barrier_semaphore()
@@ -94,9 +91,8 @@
     pl.semaphore_signal(barrier, inc=1, device_id=at_line(before), device_id_type=MESH)
     for r in range(1, 8):
         pl.semaphore_signal(barrier, inc=1, device_id=member((me + r) % 8), device_id_type=MESH)
-    for r in range(1, 4):
-        pl.semaphore_signal(barrier, inc=1, device_id=at_y((y + r) % 4), device_id_type=MESH)
-        pl.semaphore_signal(barrier, inc=1, device_id=at_z((z + r) % 4), device_id_type=MESH)
+    for r in range(1, 16):
+        pl.semaphore_signal(barrier, inc=1, device_id=peer((mine + r) % 16), device_id_type=MESH)
 
     def halo_copy(g):
         cols = pl.ds(pl.multiple_of(g * GW, GW), GW)
@@ -113,15 +109,10 @@
             src_ref=agg_v.at[rows(c * 8 + to, AGG), :], dst_ref=got_v.at[rows(c * 8 + me, AGG), :],
             send_sem=send1.at[c, r], recv_sem=recv1.at[c, r], device_id=member(to), device_id_type=MESH)
 
-    def y_copy(c, r):
+    def group_copy(c, r):
         return pltpu.make_async_remote_copy(
-            src_ref=total_v.at[rows(c, AGG), :], dst_ref=ys_v.at[rows(c * 4 + y, AGG), :],
-            send_sem=sendy.at[c, r], recv_sem=recvy.at[c, r], device_id=at_y((y + r) % 4), device_id_type=MESH)
-
-    def z_copy(c, r):
-        return pltpu.make_async_remote_copy(
-            src_ref=ytotal_v.at[rows(c, AGG), :], dst_ref=zs_v.at[rows(c * 4 + z, AGG), :],
-            send_sem=sendz.at[c, r], recv_sem=recvz.at[c, r], device_id=at_z((z + r) % 4), device_id_type=MESH)
+            src_ref=total_v.at[rows(c, AGG), :], dst_ref=all_v.at[rows(c * 16 + mine, AGG), :],
+            send_sem=send2.at[c, r], recv_sem=recv2.at[c, r], device_id=peer((mine + r) % 16), device_id_type=MESH)
 
     def last_copy(c, r):
         to = (me + r) % 8
@@ -131,7 +122,6 @@
 
     agg_v[...] = jnp.zeros_like(agg_v)
     total_v[...] = jnp.zeros_like(total_v)
-    ytotal_v[...] = jnp.zeros_like(ytotal_v)
     proj_v[...] = jnp.zeros_like(proj_v)
     for cp in ones[:2]:
         cp.wait()
@@ -181,7 +171,7 @@
         return 0
 
     conv_later(0)
-    pl.semaphore_wait(barrier, 15)
+    pl.semaphore_wait(barrier, 24)
     for g in range(G):
         halo_copy(g).start()
 
@@ -312,53 +302,28 @@
         for k in range(1, 8):
             d = d + dsums(got_v, c * 8 + k)
         put(total_v, c, 2 * N, 8, d)
-        put(ys_v, c * 4 + y, 2 * N, 8, d)
+        put(all_v, c * 16 + mine, 2 * N, 8, d)
         for half in range(2):
             rate = rates(c, half)
             s = jnp.zeros((N, LANES), f32)
             for k in range(8):
                 s = advance(s, got_v, c * 8 + k, rate, half)
             put(total_v, c, half * N, N, s)
-            put(ys_v, c * 4 + y, half * N, N, s)
-        for r in range(1, 4):
-            y_copy(c, r).start()
-
-    def after_y(c):
-        for r in range(1, 4):
-            y_copy(c, r).wait_recv()
-        d = dsums(ys_v, c * 4)
-        pre = jnp.where(y > 0, d, 0.0)
-        for k in range(1, 4):
-            now = dsums(ys_v, c * 4 + k)
-            d = d + now
-            pre = pre + jnp.where(y > k, now, 0.0)
-        put(part_v, c, 2 * N, 8, pre)
-        put(ytotal_v, c, 2 * N, 8, d)
-        put(zs_v, c * 4 + z, 2 * N, 8, d)
+            put(all_v, c * 16 + mine, half * N, N, s)
+        for r in range(1, 16):
+            group_copy(c, r).start()
+
+    def after_group(c):
+        for r in range(1, 16):
+            group_copy(c, r).wait_recv()
         for half in range(2):
             rate = rates(c, half)
             s = jnp.zeros((N, LANES), f32)
-            pre = s
-            for k in range(4):
-                s = advance(s, ys_v, c * 4 + k, rate, half)
-                pre = jnp.where(y > k, s, pre)
-            put(part_v, c, half * N, N, pre)
-            put(ytotal_v, c, half * N, N, s)
-            put(zs_v, c * 4 + z, half * N, N, s)
-        for r in range(1, 4):
-            z_copy(c, r).start()
-
-    def after_z(c):
-        for r in range(1, 4):
-            z_copy(c, r).wait_recv()
-        for half in range(2):
-            rate = rates(c, half)
-            s = jnp.zeros((N, LANES), f32)
-            pre = s
-            for k in range(3):
-                s = advance(s, zs_v, c * 4 + k, rate, half)
-                pre = jnp.where(z > k, s, pre)
-            s = advance(pre, part_v, c, rate, half)
+            before_mine = s
+            for k in range(15):
+                s = advance(s, all_v, c * 16 + k, rate, half)
+                before_mine = jnp.where(mine > k, s, before_mine)
+            s = before_mine
             for k in range(8):
                 back_v[pl.ds(pl.multiple_of((c * 8 + k) * 2 * N + half * N, 8), N), :] = s
                 if k < 7:
@@ -426,15 +391,13 @@
     def pair(work, lo, hi):
         def body(p, _):
             work(p, 0)
-            if hi > 2 and lo < C + 2:
-                pl.when((p >= 2) & (p < C + 2))(lambda: after_y(p - 2))
             work(p, 1)
             if hi <= C:
                 send_first(p)
             if hi > 1 and lo <= C:
                 pl.when((p >= 1) & (p <= C))(lambda: after_first(p - 1))
             if hi > 2 and lo < C + 2:
-                pl.when((p >= 2) & (p < C + 2))(lambda: after_z(p - 2))
+                pl.when((p >= 2) & (p < C + 2))(lambda: after_group(p - 2))
             return 0
 
         lax.fori_loop(lo, hi, body, 0)
@@ -448,9 +411,8 @@
         for r in range(1, 8):
             first_copy(c, r).wait_send()
             last_copy(c, r).wait_send()
-        for r in range(1, 4):
-            y_copy(c, r).wait_send()
-            z_copy(c, r).wait_send()
+        for r in range(1, 16):
+            group_copy(c, r).wait_send()
     for g in range(G):
         halo_copy(g).wait_send()
         out_copy(g).wait()
@@ -477,10 +439,9 @@
             vmem((T, R + 2 * N), f32), vmem((G // 2 + 1, ROWS, LANES), f32), vmem((G // 2 + 1, ROWS, LANES), f32),
             vmem((G, ROWS, LANES), f32), vmem((G // 2, ROWS, LANES), f32), vmem((G, T, GW), f32),
             vmem((C * 8 * AGG, LANES), f32), vmem((C * 8 * AGG, LANES), f32), vmem((C * AGG, LANES), f32),
-            vmem((C * 4 * AGG, LANES), f32), vmem((C * AGG, LANES), f32), vmem((C * AGG, LANES), f32),
-            vmem((C * 4 * AGG, LANES), f32), vmem((C * 8 * 2 * N, LANES), f32), vmem((C * 8 * 2 * N, LANES), f32),
+            vmem((C * 16 * AGG, LANES), f32), vmem((C * 8 * 2 * N, LANES), f32), vmem((C * 8 * 2 * N, LANES), f32),
             dma((3, G)), dma((5,)), dma((G,)), dma((G,)), dma((G,)),
-            dma((C, 8)), dma((C, 8)), dma((C, 4)), dma((C, 4)), dma((C, 4)), dma((C, 4)), dma((C, 8)), dma((C, 8))],
+            dma((C, 8)), dma((C, 8)), dma((C, 16)), dma((C, 16)), dma((C, 8)), dma((C, 8))],
         compiler_params=pltpu.CompilerParams(collective_id=0, has_side_effects=True, vmem_limit_bytes=52 * 2**20),
     )(*(pltpu.with_memory_space_constraint(v, pltpu.HBM) for v in (
         x_in, conv_weight, conv_bias.reshape(1, E), x_proj.T, dt_proj, dt_bias.reshape(1, E), decay_rates,

time: 64.2 us -> 62.1 us (0.967)
  Pallas kernels: 61.7 us -> 59.6 us
    pallas_call x1, Pallas kernels: 61.7 us -> 59.6 us  [local(): pl.pallas_call(kernel, name='selective_scan', out_shape=pltpu.VMEM((T, E)...]
where the time goes in v6:
time: 62.1 us; the launch traced here: 62 us
  Pallas kernels  59.6 us (96%)
  other arithmetic  2.34 us (4%)
    pallas_call x1, Pallas kernels, local(): pl.pallas_call(kernel, name='selective_scan', out_shape=pltpu.VMEM((T, E)...  59.6 us
    convert_element_type x1, other arithmetic, local(): return (y * (gate * (0.5 * jnp.tanh(0.5 * gate) + 0.5))).astype(bf16)  2.34 us

profile of v6, /device:TPU:1, one launch (start us, length us, event | category | flops | bytes accessed | tf_op | source)
XLA Modules:
  0.0 62.0 jit_solution(17172784108873009077)
XLA Ops:
  0.0 0.0 copy-start
  0.0 59.6 %selective_scan.1 = f32[128,8192]{1,0:T(8,128)S(1)} custom-call(bf16[128,8192]{1,0:T(8,128)(2,1)} %x_hbm.1, f32[4,8192]{1,0:T(4,128)} %cw_hbm.1, f32[1,8192]{1,0:T(1,128)} %bitcast.5, bf16[288,8192]{1,0:T(8,128)(2,1)} %bitcast.4, bf16[256,8192]{1,0:T(8,128)(2,1)} %dp_hbm.1, f32[1,8192]{1,0:T(1,128)} %bitcast.6, f32[16,8192]{1,0:T(8,128)} %a_hbm.1, ...), custom_call_target="tpu_custom_call" | custom-call | tf_op jit(solution)/shard_map/selective_scan/pallas_call | solution.py:428
  59.6 0.0 copy-done
  59.6 2.3 %fusion.4 = bf16[128,8192]{1,0:T(8,128)(2,1)} fusion(f32[128,8192]{1,0:T(8,128)S(1)} %selective_scan.1, bf16[128,8192]{1,0:T(8,128)(2,1)S(1)} %copy-done), kind=kLoop, calls=%fused_computation.6 | loop fusion | flops 7340032 | bytes 8388608 | tf_op jit(solution)/shard_map/convert_element_type | solution.py:450
Async XLA Ops:
  0.0 59.6 %copy-start = (bf16[128,8192]{1,0:T(8,128)(2,1)S(1)}, bf16[128,8192]{1,0:T(8,128)(2,1)}, u32[]{:S(2)}) copy-start(bf16[128,8192]{1,0:T(8,128)(2,1)} %param.10) | copy-start | bytes 6291460

commit v7 on v6

--- a/solution.py
+++ b/solution.py
@@ -130,14 +130,14 @@
         wch_v[g, pl.ds(j, KW, stride=J), :] = cw_v[:, cols]
         wch_v[g, KW * J + j:KW * J + j + 1, :] = cb_v[:, cols]
 
-    def conv_tokens(g, k):
+    def conv_tokens(g, k, slot=0):
         w = [wch_v[g, i * J:(i + 1) * J, :] for i in range(KW + 1)]
         for tt in range(16):
             r = pl.multiple_of((k * 16 + tt) * J, J)
             acc = w[KW]
             for i in range(KW):
                 acc = acc + w[i] * xch_v[g, pl.ds(r + (HALO - KW + 1 + i) * J, J), :]
-            dch_v[0, pl.ds(r, J), :] = silu(acc)
+            dch_v[slot, pl.ds(r, J), :] = silu(acc)
 
     def conv_later(g):
         @pl.when(g + AHEAD < G)
@@ -157,17 +157,23 @@
             late = dch_v[0, pl.ds(16 * J + j, T - 16, stride=J), :]
             u_v[g, 16:T, j * LANES:(j + 1) * LANES] = late.astype(bf16)
 
-    def conv_first(g, _):
-        in_copy(2, g).start()
-        halo_copy(g).wait_recv()
-        for j in range(J):
-            halo = halo_v[g, :, j * LANES:(j + 1) * LANES].astype(f32)
-            xch_v[g, pl.ds(j, HALO, stride=J), :] = jnp.where(line > 0, halo, 0.0)
-        conv_tokens(g, 0)
-        for j in range(J):
-            u_v[g, 0:16, j * LANES:(j + 1) * LANES] = dch_v[0, pl.ds(j, 16, stride=J), :].astype(bf16)
-        in_copy(1, g).wait()
-        proj_v[...] += lax.dot_general(u_v[g], xp_v[g], (((1,), (1,)), ((), ())), preferred_element_type=f32)
+    def conv_first(pair_of_groups, _):
+        two = [(2 * pair_of_groups + slot, slot) for slot in range(2)]
+        for g, slot in two:
+            in_copy(2, g).start()
+            halo_copy(g).wait_recv()
+            in_copy(1, g).wait()
+        for g, slot in two:
+            for j in range(J):
+                halo = halo_v[g, :, j * LANES:(j + 1) * LANES].astype(f32)
+                xch_v[g, pl.ds(j, HALO, stride=J), :] = jnp.where(line > 0, halo, 0.0)
+            conv_tokens(g, 0, slot)
+            for j in range(J):
+                early = dch_v[slot, pl.ds(j, 16, stride=J), :]
+                u_v[g, 0:16, j * LANES:(j + 1) * LANES] = early.astype(bf16)
+        proj = [lax.dot_general(u_v[g], xp_v[g], (((1,), (1,)), ((), ())), preferred_element_type=f32)
+                for g, slot in two]
+        proj_v[...] += proj[0] + proj[1]
         return 0
 
     conv_later(0)
@@ -184,7 +190,7 @@
         cp.wait()
     for q in range(E // LANES):
         ach_v[q // J, pl.ds(q % J, N, stride=J), :] = a_v[:, q * LANES:(q + 1) * LANES] * -LOG2E
-    lax.fori_loop(0, G, conv_first, 0)
+    lax.fori_loop(0, G // 2, conv_first, 0)
 
     row = lax.broadcasted_iota(jnp.int32, (256, 16), 0)
     col = lax.broadcasted_iota(jnp.int32, (256, 16), 1)

time: 62.1 us -> 62 us (level)
  no operation moved by 1% of the time
where the time goes in v7:
time: 62 us; the launch traced here: 61.9 us
  Pallas kernels  59.5 us (96%)
  other arithmetic  2.34 us (4%)
    pallas_call x1, Pallas kernels, local(): pl.pallas_call(kernel, name='selective_scan', out_shape=pltpu.VMEM((T, E)...  59.5 us
    convert_element_type x1, other arithmetic, local(): return (y * (gate * (0.5 * jnp.tanh(0.5 * gate) + 0.5))).astype(bf16)  2.34 us

profile of v7, /device:TPU:1, one launch (start us, length us, event | category | flops | bytes accessed | tf_op | source)
XLA Modules:
  0.0 61.9 jit_solution(10541197400973880615)
XLA Ops:
  0.0 0.0 copy-start
  0.0 59.5 %selective_scan.1 = f32[128,8192]{1,0:T(8,128)S(1)} custom-call(bf16[128,8192]{1,0:T(8,128)(2,1)} %x_hbm.1, f32[4,8192]{1,0:T(4,128)} %cw_hbm.1, f32[1,8192]{1,0:T(1,128)} %bitcast.5, bf16[288,8192]{1,0:T(8,128)(2,1)} %bitcast.4, bf16[256,8192]{1,0:T(8,128)(2,1)} %dp_hbm.1, f32[1,8192]{1,0:T(1,128)} %bitcast.6, f32[16,8192]{1,0:T(8,128)} %a_hbm.1, ...), custom_call_target="tpu_custom_call" | custom-call | tf_op jit(solution)/shard_map/selective_scan/pallas_call | solution.py:434
  59.5 0.0 copy-done
  59.5 2.3 %fusion.4 = bf16[128,8192]{1,0:T(8,128)(2,1)} fusion(f32[128,8192]{1,0:T(8,128)S(1)} %selective_scan.1, bf16[128,8192]{1,0:T(8,128)(2,1)S(1)} %copy-done), kind=kLoop, calls=%fused_computation.6 | loop fusion | flops 7340032 | bytes 8388608 | tf_op jit(solution)/shard_map/convert_element_type | solution.py:456
Async XLA Ops:
  0.0 59.5 %copy-start = (bf16[128,8192]{1,0:T(8,128)(2,1)S(1)}, bf16[128,8192]{1,0:T(8,128)(2,1)}, u32[]{:S(2)}) copy-start(bf16[128,8192]{1,0:T(8,128)(2,1)} %param.10) | copy-start | bytes 6291460

commit v8 on v7

--- a/solution.py
+++ b/solution.py
@@ -26,6 +26,7 @@
 C = G // 2
 AGG = 40
 HALO = 16
+WIRE = 48
 
 
 def silu(v):
@@ -103,6 +104,9 @@
     def rows(index, count):
         return pl.ds(pl.multiple_of(index * count, 8), count)
 
+    def wire(slot, row, count):
+        return pl.ds(pl.multiple_of(slot * WIRE + row, 16), count)
+
     def first_copy(c, r):
         to = (me + r) % 8
         return pltpu.make_async_remote_copy(
@@ -111,7 +115,7 @@
 
     def group_copy(c, r):
         return pltpu.make_async_remote_copy(
-            src_ref=total_v.at[rows(c, AGG), :], dst_ref=all_v.at[rows(c * 16 + mine, AGG), :],
+            src_ref=total_v.at[wire(c, 0, WIRE), :], dst_ref=all_v.at[wire(c * 16 + mine, 0, WIRE), :],
             send_sem=send2.at[c, r], recv_sem=recv2.at[c, r], device_id=peer((mine + r) % 16), device_id_type=MESH)
 
     def last_copy(c, r):
@@ -293,9 +297,6 @@
     def dsums(ref, slot):
         return ref[pl.ds(pl.multiple_of(slot * AGG + 2 * N, 8), 8), :]
 
-    def put(ref, slot, row, count, value):
-        ref[pl.ds(pl.multiple_of(slot * AGG + row, 8), count), :] = value
-
     def send_first(c):
         got_v[rows(c * 8 + me, AGG), :] = agg_v[rows(c * 8 + me, AGG), :]
         for r in range(1, 8):
@@ -307,15 +308,16 @@
         d = dsums(got_v, c * 8)
         for k in range(1, 8):
             d = d + dsums(got_v, c * 8 + k)
-        put(total_v, c, 2 * N, 8, d)
-        put(all_v, c * 16 + mine, 2 * N, 8, d)
+        d = jnp.concatenate([part[0:2] for part in split3(d)] + [jnp.zeros((10, LANES), f32)], axis=0).astype(bf16)
+        total_v[wire(c, 2 * N, N), :] = d
+        all_v[wire(c * 16 + mine, 2 * N, N), :] = d
         for half in range(2):
             rate = rates(c, half)
             s = jnp.zeros((N, LANES), f32)
             for k in range(8):
                 s = advance(s, got_v, c * 8 + k, rate, half)
-            put(total_v, c, half * N, N, s)
-            put(all_v, c * 16 + mine, half * N, N, s)
+            total_v[wire(c, half * N, N), :] = s.astype(bf16)
+            all_v[wire(c * 16 + mine, half * N, N), :] = s.astype(bf16)
         for r in range(1, 16):
             group_copy(c, r).start()
 
@@ -327,7 +329,9 @@
             s = jnp.zeros((N, LANES), f32)
             before_mine = s
             for k in range(15):
-                s = advance(s, all_v, c * 16 + k, rate, half)
+                d = all_v[wire(c * 16 + k, 2 * N, N), :].astype(f32)
+                d = d[half:half + 1] + d[2 + half:3 + half] + d[4 + half:5 + half]
+                s = jnp.exp2(d * rate) * s + all_v[wire(c * 16 + k, half * N, N), :].astype(f32)
                 before_mine = jnp.where(mine > k, s, before_mine)
             s = before_mine
             for k in range(8):
@@ -444,8 +448,8 @@
             vmem((G, T, GW), bf16), vmem((T * N, LANES), f32), vmem((T * N, LANES), f32), vmem((G, N * J, LANES), f32),
             vmem((T, R + 2 * N), f32), vmem((G // 2 + 1, ROWS, LANES), f32), vmem((G // 2 + 1, ROWS, LANES), f32),
             vmem((G, ROWS, LANES), f32), vmem((G // 2, ROWS, LANES), f32), vmem((G, T, GW), f32),
-            vmem((C * 8 * AGG, LANES), f32), vmem((C * 8 * AGG, LANES), f32), vmem((C * AGG, LANES), f32),
-            vmem((C * 16 * AGG, LANES), f32), vmem((C * 8 * 2 * N, LANES), f32), vmem((C * 8 * 2 * N, LANES), f32),
+            vmem((C * 8 * AGG, LANES), f32), vmem((C * 8 * AGG, LANES), f32), vmem((C * WIRE, LANES), bf16),
+            vmem((C * 16 * WIRE, LANES), bf16), vmem((C * 8 * 2 * N, LANES), f32), vmem((C * 8 * 2 * N, LANES), f32),
             dma((3, G)), dma((5,)), dma((G,)), dma((G,)), dma((G,)),
             dma((C, 8)), dma((C, 8)), dma((C, 16)), dma((C, 16)), dma((C, 8)), dma((C, 8))],
         compiler_params=pltpu.CompilerParams(collective_id=0, has_side_effects=True, vmem_limit_bytes=52 * 2**20),

time: 62 us -> 60 us (0.968)
  Pallas kernels: 59.5 us -> 57.6 us
    pallas_call x1, Pallas kernels: 59.5 us -> 57.6 us  [local(): pl.pallas_call(kernel, name='selective_scan', out_shape=pltpu.VMEM((T, E)...]
where the time goes in v8:
time: 60 us; the launch traced here: 59.9 us
  Pallas kernels  57.6 us (96%)
  other arithmetic  2.34 us (4%)
    pallas_call x1, Pallas kernels, local(): pl.pallas_call(kernel, name='selective_scan', out_shape=pltpu.VMEM((T, E)...  57.6 us
    convert_element_type x1, other arithmetic, local(): return (y * (gate * (0.5 * jnp.tanh(0.5 * gate) + 0.5))).astype(bf16)  2.34 us

profile of v8, /device:TPU:1, one launch (start us, length us, event | category | flops | bytes accessed | tf_op | source)
XLA Modules:
  0.0 59.9 jit_solution(12528714338367001158)
XLA Ops:
  0.0 0.0 copy-start
  0.0 57.6 %selective_scan.1 = f32[128,8192]{1,0:T(8,128)S(1)} custom-call(bf16[128,8192]{1,0:T(8,128)(2,1)} %x_hbm.1, f32[4,8192]{1,0:T(4,128)} %cw_hbm.1, f32[1,8192]{1,0:T(1,128)} %bitcast.5, bf16[288,8192]{1,0:T(8,128)(2,1)} %bitcast.4, bf16[256,8192]{1,0:T(8,128)(2,1)} %dp_hbm.1, f32[1,8192]{1,0:T(1,128)} %bitcast.6, f32[16,8192]{1,0:T(8,128)} %a_hbm.1, ...), custom_call_target="tpu_custom_call" | custom-call | tf_op jit(solution)/shard_map/selective_scan/pallas_call | solution.py:438
  57.6 0.0 copy-done
  57.6 2.3 %fusion.4 = bf16[128,8192]{1,0:T(8,128)(2,1)} fusion(f32[128,8192]{1,0:T(8,128)S(1)} %selective_scan.1, bf16[128,8192]{1,0:T(8,128)(2,1)S(1)} %copy-done), kind=kLoop, calls=%fused_computation.6 | loop fusion | flops 7340032 | bytes 8388608 | tf_op jit(solution)/shard_map/convert_element_type | solution.py:460
Async XLA Ops:
  0.0 57.6 %copy-start = (bf16[128,8192]{1,0:T(8,128)(2,1)S(1)}, bf16[128,8192]{1,0:T(8,128)(2,1)}, u32[]{:S(2)}) copy-start(bf16[128,8192]{1,0:T(8,128)(2,1)} %param.10) | copy-start | bytes 6291460
